TPU v7x, 128 devices: a whole 4x4x4 slice. The times are simulated.
128 devices in a mesh: role: 2 (over z_lo), fsdp: 64 (over z_hi, x, y, core).
Axes of the slice: x: 4, y: 4, z: 4 (z_hi: 2, z_lo: 2; z = z_hi * 2 + z_lo), core: 2. Of those that a mesh axis runs over, the one named last changes fastest.
Arguments:
- queries: bfloat16 [256, 2, 4096], P('fsdp'), may hold values from -504 to 504, as said below
- new_keys: bfloat16 [256, 2, 2048], P('fsdp'), may hold values from -9 to 9
- new_values: bfloat16 [256, 2, 2048], P('fsdp'), may hold values from -6 to 6
- cache_keys: bfloat16 [256, 256, 2048], P('fsdp'), may hold values from -9 to 9
- cache_values: bfloat16 [256, 256, 2048], P('fsdp'), may hold values from -6 to 6
- context_lengths: int32 [256], P('fsdp'), may hold values from 32 to 256
- rollout_rows: bfloat16 [512, 4, 5376], P(('role', 'fsdp')), may hold values from -6 to 6
- cotangents: bfloat16 [512, 4, 5376], P(('role', 'fsdp')), may hold values from -6 to 6
- rewards: float32 [512], P(('role', 'fsdp')), may hold values from 0 to 4
- prompt_keys: int32 [512], P(('role', 'fsdp')), may hold values from 0 to 7, as said below
- completion_lengths: int32 [512], P(('role', 'fsdp')), may hold values from 1 to 4
- finished_counts: int32 [128], P(('role', 'fsdp')), may hold values from 0 to 4, as said below
- gate_weight: bfloat16 [5376, 21504], P(None, 'fsdp'), may hold values from -0.078125 to 0.078125
- up_weight: bfloat16 [5376, 21504], P(None, 'fsdp'), may hold values from -0.078125 to 0.078125
- down_weight: bfloat16 [21504, 5376], P('fsdp'), may hold values from -0.0390625 to 0.0390625
Outputs:
- attended: bfloat16 [256, 2, 4096], P('fsdp')
- grad_gate: bfloat16 [5376, 21504], P('role', 'fsdp')
- grad_up: bfloat16 [5376, 21504], P('role', 'fsdp')
- grad_down: bfloat16 [21504, 5376], P('fsdp', 'role')
Inputs may be any that keep to these rules, and one draw needn't show every extreme that they name: `queries`: in the shown draw these are plain normal numbers; the array's values stay within the range below. `finished_counts`: the first 64 entries belong to the generator devices and add up to 128; the last 64 entries, those of the learner devices, are zero. A device's live slots are its first ones. `prompt_keys`: over all live slots every prompt group is named by exactly 16 samples.
All inputs are finite; a program needn't handle non-finite values.
Results may differ from a plain program's by a relative error of at most 0.0058.
Values may be sent and summed in bfloat16 or wider, within the bound.
A program may use at most 192 MiB of HBM per device.

v0:
```python
import jax
import jax.numpy as jnp
from jax import lax
from jax.sharding import PartitionSpec as P

HEADS = 32
KV_HEADS = 16
HEAD_DIM = 128
QSCALAR = 168
GROUP = 16


def from_behind(value, axis, steps):
    count = lax.axis_size(axis)
    initial, last = (max(0, -steps), min(count, count - steps))
    return lax.ppermute(value, axis, [(source, source + steps) for source in range(initial, last)])


def gelu_pair(values):
    inner_arg = 0.7978845608028654 * (values + 0.044715 * values * values * values)
    tangent = jnp.tanh(inner_arg)
    result = 0.5 * values * (1.0 + tangent)
    slope_value = 0.5 * (1.0 + tangent) + 0.5 * values * (
        1.0 - tangent * tangent
    ) * 0.7978845608028654 * (1.0 + 3.0 * 0.044715 * values * values)
    return (result, slope_value)


def attend_block(queries, new_keys, new_values, cache_keys, cache_values, context_lengths):
    sample_count, cache_length, kv_width = cache_keys.shape
    grouped = HEADS // KV_HEADS
    query_block = queries.reshape(sample_count, 2, KV_HEADS, grouped, HEAD_DIM)
    old_keys = cache_keys.reshape(sample_count, cache_length, KV_HEADS, HEAD_DIM)
    old_values = cache_values.reshape(sample_count, cache_length, KV_HEADS, HEAD_DIM)
    fresh_keys = new_keys.reshape(sample_count, 2, KV_HEADS, HEAD_DIM)
    fresh_values = new_values.reshape(sample_count, 2, KV_HEADS, HEAD_DIM)
    score_scale = float(QSCALAR) ** (-0.5)
    cache_scores = (
        jnp.einsum("btkgd,bpkd->btkgp", query_block, old_keys, preferred_element_type=jnp.float32)
        * score_scale
    )
    fresh_scores = (
        jnp.einsum("btkgd,bskd->btkgs", query_block, fresh_keys, preferred_element_type=jnp.float32)
        * score_scale
    )
    cache_mask = jnp.arange(cache_length)[None, :] < context_lengths[:, None]
    step_mask = jnp.arange(2)[None, :] <= jnp.arange(2)[:, None]
    cache_scores = jnp.where(cache_mask[:, None, None, None, :], cache_scores, -1e30)
    fresh_scores = jnp.where(step_mask[None, :, None, None, :], fresh_scores, -1e30)
    row_max = jnp.maximum(
        jnp.max(cache_scores, axis=-1, keepdims=True), jnp.max(fresh_scores, axis=-1, keepdims=True)
    )
    cache_weights = jnp.exp(cache_scores - row_max)
    fresh_weights = jnp.exp(fresh_scores - row_max)
    total_weight = jnp.sum(cache_weights, axis=-1, keepdims=True) + jnp.sum(
        fresh_weights, axis=-1, keepdims=True
    )
    cache_probs = (cache_weights / total_weight).astype(jnp.bfloat16)
    fresh_probs = (fresh_weights / total_weight).astype(jnp.bfloat16)
    combined = jnp.einsum(
        "btkgp,bpkd->btkgd", cache_probs, old_values, preferred_element_type=jnp.float32
    )
    combined = combined + jnp.einsum(
        "btkgs,bskd->btkgd", fresh_probs, fresh_values, preferred_element_type=jnp.float32
    )
    return combined.reshape(sample_count, 2, HEADS * HEAD_DIM).astype(jnp.bfloat16)


def local(
    queries,
    new_keys,
    new_values,
    cache_keys,
    cache_values,
    context_lengths,
    rollout_rows,
    cotangents,
    rewards,
    prompt_keys,
    completion_lengths,
    finished_counts,
    gate_weight,
    up_weight,
    down_weight,
):
    attended = attend_block(
        queries, new_keys, new_values, cache_keys, cache_values, context_lengths
    )
    role_index = lax.axis_index("role")
    slot_count = rewards.shape[0]
    token_count = rollout_rows.shape[1]
    model_width = gate_weight.shape[0]
    half_width = model_width // 2
    group_count = lax.axis_size("fsdp") * slot_count // (2 * GROUP)
    live_slot = jnp.arange(slot_count) < finished_counts[0]
    member = (
        (prompt_keys[:, None] == jnp.arange(group_count)[None, :]) & live_slot[:, None]
    ).astype(jnp.float32)
    group_sum, group_sq = lax.psum(
        (
            jnp.sum(member * rewards[:, None], axis=0),
            jnp.sum(member * (rewards * rewards)[:, None], axis=0),
        ),
        "fsdp",
    )
    group_mean = group_sum / GROUP
    spread = group_sq / GROUP - group_mean * group_mean
    denominator = jnp.maximum(jnp.sqrt(jnp.maximum(spread, 0.0)), 1.0)
    slot_mean = jnp.sum(member * group_mean[None, :], axis=1)
    slot_scale = jnp.sum(member * denominator[None, :], axis=1)
    advantage = jnp.where(
        live_slot, (rewards - slot_mean) / jnp.where(live_slot, slot_scale, 1.0), 0.0
    )
    lengths_float = completion_lengths.astype(jnp.float32)
    token_live = jnp.arange(token_count)[None, :] < completion_lengths[:, None]
    token_weight = jnp.where(token_live, advantage[:, None] / lengths_float[:, None], 0.0)
    scaled = (cotangents.astype(jnp.float32) * token_weight[:, :, None]).astype(jnp.bfloat16)
    arrived_rows, arrived_scaled = from_behind((rollout_rows, scaled), "role", 1)
    contract = (((0,), (0,)), ((), ()))
    row_block = lax.all_gather(arrived_rows, "fsdp", axis=0, tiled=True).reshape(-1, model_width)
    scaled_block = lax.all_gather(arrived_scaled, "fsdp", axis=0, tiled=True).reshape(
        -1, model_width
    )
    gate_value = jnp.dot(row_block, gate_weight, preferred_element_type=jnp.float32)
    up_value = jnp.dot(row_block, up_weight, preferred_element_type=jnp.float32)
    active, slope_value = gelu_pair(gate_value)
    hidden = (active * up_value).astype(jnp.bfloat16)
    back_grad = lax.dot_general(
        scaled_block, down_weight, (((1,), (1,)), ((), ())), preferred_element_type=jnp.float32
    )
    d_gate = (back_grad * up_value * slope_value).astype(jnp.bfloat16)
    d_up = (back_grad * active).astype(jnp.bfloat16)
    grad_gate = lax.dot_general(
        row_block, d_gate, contract, preferred_element_type=jnp.float32
    ).astype(jnp.bfloat16)
    grad_up = lax.dot_general(row_block, d_up, contract, preferred_element_type=jnp.float32).astype(
        jnp.bfloat16
    )
    grad_down = lax.dot_general(
        hidden, scaled_block, contract, preferred_element_type=jnp.float32
    ).astype(jnp.bfloat16)
    upper = (grad_gate[:half_width], grad_up[:half_width], grad_down[:, :half_width])
    received = from_behind((upper[0], upper[1], upper[2]), "role", -1)
    on_generator = role_index == 0
    final_gate = jnp.where(on_generator, received[0], grad_gate[half_width:])
    final_up = jnp.where(on_generator, received[1], grad_up[half_width:])
    final_down = jnp.where(on_generator, received[2], grad_down[:, half_width:])
    return (attended, final_gate, final_up, final_down)


def solution(mesh):
    return jax.shard_map(
        local,
        mesh=mesh,
        in_specs=(
            P("fsdp", None, None),
            P("fsdp", None, None),
            P("fsdp", None, None),
            P("fsdp", None, None),
            P("fsdp", None, None),
            P("fsdp"),
            P(("role", "fsdp"), None, None),
            P(("role", "fsdp"), None, None),
            P(("role", "fsdp")),
            P(("role", "fsdp")),
            P(("role", "fsdp")),
            P(("role", "fsdp")),
            P(None, "fsdp"),
            P(None, "fsdp"),
            P("fsdp", None),
        ),
        out_specs=(P("fsdp", None, None), P("role", "fsdp"), P("role", "fsdp"), P("fsdp", "role")),
        check_vma=False,
    )
```

profile of v0, /device:TPU:1, one launch (start us, length us, event | category | flops | bytes accessed | tf_op | source)
XLA Modules:
  0.0 444.9 jit_solution(16163402019603712597)
XLA Ops:
  7.2 4.4 collective-permute-start.1
  11.6 3.3 collective-permute-done.1
  17.8 165.0 %all-reduce = (f32[8]{0:T(128)S(1)}, f32[8]{0:T(128)S(1)}) all-reduce(f32[8]{0:T(128)S(1)} %get-tuple-element.6, f32[8]{0:T(128)S(1)} %get-tuple-element.7), channel_id=1, replica_groups=mesh['role'=2,'fsdp'=64] {'fsdp'}, use_global_device_ids=true, to_apply=%region_5.6 | all-reduce | flops 16 | bytes 128 | tf_op jit(solution)/shard_map/psum | solution.py:99
  185.5 3.5 collective-permute-start
  189.0 2.3 collective-permute-done
  192.9 2.0 fusion.40
  195.3 3.6 copy.93
  202.4 3.6 copy.94
  206.2 2.7 bitcast_bitcast_fusion
  209.0 17.0 %reshape.125 = bf16[1024,5376]{1,0:T(8,128)(2,1)} reshape(bf16[256,4,5376]{2,1,0:T(4,128)(2,1)} %all-gather.5.cloned.1.call-done) | data formatting | bytes 22020096 | tf_op jit(solution)/shard_map/reshape | solution.py:120
  226.0 7.9 %fusion.67 = f32[1024,336]{0,1:T(8,128)S(1)} fusion(bf16[1024,5376]{1,0:T(8,128)(2,1)} %reshape.125, bf16[5376,336]{0,1:T(8,128)(2,1)} %param.27), kind=kOutput, calls=%fused_computation.84 | convolution fusion | flops 3699376128 | bytes 15998976 | tf_op jit(solution)/shard_map/dot_general | solution.py:124
  235.5 5.0 %fusion.66 = f32[1024,336]{0,1:T(8,128)} fusion(bf16[1024,5376]{1,0:T(8,128)(2,1)S(1)} %copy-done.2, bf16[5376,336]{0,1:T(8,128)(2,1)S(1)} %copy-done.12), kind=kOutput, calls=%fused_computation.83 | convolution fusion | flops 3699376128 | bytes 15998976 | tf_op jit(solution)/shard_map/dot_general | solution.py:125
  240.4 44.6 %all-gather.3.cloned.1.call-done = bf16[256,4,5376]{2,1,0:T(4,128)(2,1)} async-done(((bf16[4,4,5376]{2,1,0:T(4,128)(2,1)}), bf16[256,4,5376]{2,1,0:T(4,128)(2,1)}) %all-gather.3.cloned.1.call-update) | async-done | bytes 11010064 | tf_op jit(solution)/shard_map/all_gather | solution.py:121
  285.1 17.0 %reshape.124 = bf16[1024,5376]{1,0:T(8,128)(2,1)} reshape(bf16[256,4,5376]{2,1,0:T(4,128)(2,1)} %all-gather.3.cloned.1.call-done) | data formatting | bytes 22020096 | tf_op jit(solution)/shard_map/reshape | solution.py:121
  302.1 8.9 %convolution_convert_fusion = bf16[336,5376]{1,0:T(8,128)(2,1)S(1)} fusion(bf16[1024,5376]{1,0:T(8,128)(2,1)} %reshape.124, f32[1024,336]{0,1:T(8,128)} %fusion.66, f32[1024,336]{0,1:T(8,128)S(1)} %fusion.67), kind=kOutput, calls=%fused_computation | convolution fusion | flops 3704623104 | bytes 17375232 | tf_op jit(solution)/shard_map/dot_general | solution.py:139
  315.8 6.7 %fusion.65 = f32[1024,336]{0,1:T(8,128)S(1)} fusion(bf16[1024,5376]{1,0:T(8,128)(2,1)S(1)} %copy-done.3, bf16[336,5376]{1,0:T(8,128)(2,1)} %param.29), kind=kOutput, calls=%fused_computation.82 | convolution fusion | flops 3699376128 | bytes 15998976 | tf_op jit(solution)/shard_map/dot_general | solution.py:128
  322.5 4.7 %fusion.1 = bf16[5376,336]{0,1:T(8,128)(2,1)S(1)} fusion(bf16[1024,5376]{1,0:T(8,128)(2,1)S(1)} %bitcast.62, f32[1024,336]{0,1:T(8,128)S(1)} %fusion.65, f32[1024,336]{0,1:T(8,128)S(1)} %copy-done.15), kind=kOutput, calls=%fused_computation.4 | convolution fusion | flops 3704623104 | bytes 17375232 | tf_op jit(solution)/shard_map/dot_general | solution.py:136
  330.9 7.3 %fusion = bf16[5376,336]{0,1:T(8,128)(2,1)S(1)} fusion(bf16[1024,5376]{1,0:T(8,128)(2,1)S(1)} %bitcast.62, f32[1024,336]{0,1:T(8,128)S(1)} %copy-done.15, f32[1024,336]{0,1:T(8,128)} %copy-done.17, f32[1024,336]{0,1:T(8,128)S(1)} %copy-done.16), kind=kOutput, calls=%fused_computation.3 | convolution fusion | flops 3708063744 | bytes 18751488 | tf_op jit(solution)/shard_map/dot_general | solution.py:133
  343.8 13.8 %collective-permute-done.4 = bf16[336,2688]{1,0:T(8,128)(2,1)S(1)} collective-permute-done((bf16[336,2688]{1,0:T(8,128)(2,1)}, bf16[336,2688]{1,0:T(8,128)(2,1)S(1)}, u32[]{:S(2)}, u32[]{:S(2)}) %collective-permute-start.4) | collective-permute-done | bytes 1806368 | tf_op jit(solution)/shard_map/ppermute | solution.py:16
  357.6 2.9 slice_select_fusion
  360.5 35.9 %collective-permute-done.3 = bf16[2688,336]{0,1:T(8,128)(2,1)} collective-permute-done((bf16[2688,336]{0,1:T(8,128)(2,1)}, bf16[2688,336]{0,1:T(8,128)(2,1)}, u32[]{:S(2)}, u32[]{:S(2)}) %collective-permute-start.3) | collective-permute-done | bytes 1806368 | tf_op jit(solution)/shard_map/ppermute | solution.py:16
  396.4 3.0 slice_select_fusion.1
  399.4 35.7 %collective-permute-done.2 = bf16[2688,336]{0,1:T(8,128)(2,1)} collective-permute-done((bf16[2688,336]{0,1:T(8,128)(2,1)}, bf16[2688,336]{0,1:T(8,128)(2,1)}, u32[]{:S(2)}, u32[]{:S(2)}) %collective-permute-start.2) | collective-permute-done | bytes 1806368 | tf_op jit(solution)/shard_map/ppermute | solution.py:16
  435.1 3.0 slice_select_fusion.2
  (83 shorter events, 26.1 us)
Async XLA Ops:
  7.2 198.8 %copy-start = (bf16[4,2,2048]{2,1,0:T(2,128)(2,1)S(1)}, bf16[4,2,2048]{2,1,0:T(2,128)(2,1)}, u32[]{:S(2)}) copy-start(bf16[4,2,2048]{2,1,0:T(2,128)(2,1)} %param.17) | copy-start | bytes 98308
  7.2 201.8 %all-gather.5.cloned.1.call-start = ((), (), s32[]{:S(2)}) async-start(), calls=%async_computation.1 | async-start | bytes 11182080 | tf_op jit(solution)/shard_map/all_gather | solution.py:120
  7.2 7.7 %collective-permute-start.1 = (bf16[4,4,5376]{2,1,0:T(4,128)(2,1)}, bf16[4,4,5376]{2,1,0:T(4,128)(2,1)S(1)}, u32[]{:S(2)}, u32[]{:S(2)}) collective-permute-start(bf16[4,4,5376]{2,1,0:T(4,128)(2,1)} %param.21), channel_id=1, source_target_pairs={{0,64},{1,65},{2,66},{3,67},{4,68},{5,69},{6,70},{7,71},{8,72},{9,... | collective-permute-start | bytes 516104 | tf_op jit(solution)/shard_map/ppermute | solution.py:16
  15.6 269.4 %all-gather.3.cloned.1.call-start = ((), (), s32[]{:S(2)}) async-start(), calls=%async_computation | async-start | bytes 11182080 | tf_op jit(solution)/shard_map/all_gather | solution.py:121
  185.5 5.8 %collective-permute-start = (bf16[4,4,5376]{2,1,0:T(4,128)(2,1)S(1)}, bf16[4,4,5376]{2,1,0:T(4,128)(2,1)S(1)}, u32[]{:S(2)}, u32[]{:S(2)}) collective-permute-start(bf16[4,4,5376]{2,1,0:T(4,128)(2,1)S(1)} %multiply_convert_fusion.4), channel_id=1, source_target_pairs={{0,64},{1,65},{2,66},{3,67},{4,68},{5,69},{6,70},{7,71},{8,72},{9,... | collective-permute-start | bytes 516104 | tf_op jit(solution)/shard_map/ppermute | solution.py:16
  195.3 3.6 copy-start.13
  226.0 8.4 %copy-start.2 = (bf16[1024,5376]{1,0:T(8,128)(2,1)S(1)}, bf16[1024,5376]{1,0:T(8,128)(2,1)}, u32[]{:S(2)}) copy-start(bf16[1024,5376]{1,0:T(8,128)(2,1)} %reshape.125) | copy-start | bytes 33030148
  226.0 9.5 %copy-start.12 = (bf16[5376,336]{0,1:T(8,128)(2,1)S(1)}, bf16[5376,336]{0,1:T(8,128)(2,1)}, u32[]{:S(2)}) copy-start(bf16[5376,336]{0,1:T(8,128)(2,1)} %param.28) | copy-start | bytes 10838020
  235.5 66.6 %copy-start.14 = (f32[1024,336]{0,1:T(8,128)}, f32[1024,336]{0,1:T(8,128)S(1)}, u32[]{:S(2)}) copy-start(f32[1024,336]{0,1:T(8,128)S(1)} %fusion.67) | copy-start | bytes 4128772
  302.1 13.7 %copy-start.3 = (bf16[1024,5376]{1,0:T(8,128)(2,1)S(1)}, bf16[1024,5376]{1,0:T(8,128)(2,1)}, u32[]{:S(2)}) copy-start(bf16[1024,5376]{1,0:T(8,128)(2,1)} %reshape.124) | copy-start | bytes 33030148
  312.9 9.6 %slice-start = ((s8[11010048]{0:T(1024)(128)(4,1)}), s8[4194304]{0:T(1024)(128)(4,1)S(1)}, s32[]{:S(2)}) async-start(s8[11010048]{0:T(1024)(128)(4,1)} %bitcast.61), calls=%async_computation.2 | async-start | bytes 8388608
  314.2 8.3 %slice-start.1 = ((s8[11010048]{0:T(1024)(128)(4,1)}), s8[4194304]{0:T(1024)(128)(4,1)S(1)}, s32[]{:S(2)}) async-start(s8[11010048]{0:T(1024)(128)(4,1)} %bitcast.61), calls=%async_computation.3 | async-start | bytes 8388608
  314.2 8.3 %slice-start.2 = ((s8[11010048]{0:T(1024)(128)(4,1)}), s8[2621440]{0:T(1024)(128)(4,1)S(1)}, s32[]{:S(2)}) async-start(s8[11010048]{0:T(1024)(128)(4,1)} %bitcast.61), calls=%async_computation.4 | async-start | bytes 5242880
  314.2 8.3 %copy-start.15 = (f32[1024,336]{0,1:T(8,128)S(1)}, f32[1024,336]{0,1:T(8,128)}, u32[]{:S(2)}) copy-start(f32[1024,336]{0,1:T(8,128)} %copy-done.14) | copy-start | bytes 4128772
  314.2 43.4 %collective-permute-start.4 = (bf16[336,2688]{1,0:T(8,128)(2,1)}, bf16[336,2688]{1,0:T(8,128)(2,1)S(1)}, u32[]{:S(2)}, u32[]{:S(2)}) collective-permute-start(bf16[336,2688]{1,0:T(8,128)(2,1)} %slice.28), channel_id=1, source_target_pairs={{64,0},{65,1},{66,2},{67,3},{68,4},{69,5},{70,6},{71,7},{72,8},{73... | collective-permute-start | bytes 5419016 | tf_op jit(solution)/shard_map/ppermute | solution.py:16
  322.5 4.7 %copy-start.17 = (f32[1024,336]{0,1:T(8,128)}, f32[1024,336]{0,1:T(8,128)S(1)}, u32[]{:S(2)}) copy-start(f32[1024,336]{0,1:T(8,128)S(1)} %fusion.65) | copy-start | bytes 4128772
  327.2 3.7 copy-start.16
  329.6 66.8 %collective-permute-start.3 = (bf16[2688,336]{0,1:T(8,128)(2,1)}, bf16[2688,336]{0,1:T(8,128)(2,1)}, u32[]{:S(2)}, u32[]{:S(2)}) collective-permute-start(bf16[2688,336]{0,1:T(8,128)(2,1)} %slice.26), channel_id=1, source_target_pairs={{64,0},{65,1},{66,2},{67,3},{68,4},{69,5},{70,6},{71,7},{72,8},{73... | collective-permute-start | bytes 5419016 | tf_op jit(solution)/shard_map/ppermute | solution.py:16
  330.9 11.0 %copy-start.4 = (bf16[4,256,16,128,1]{3,2,1,0,4:T(8,128)(2,1)S(1)}, bf16[4,256,16,128,1]{3,2,1,0,4:T(8,128)(2,1)}, u32[]{:S(2)}) copy-start(bf16[4,256,16,128,1]{3,2,1,0,4:T(8,128)(2,1)} %bitcast_bitcast_fusion) | copy-start | bytes 12582916
  338.2 2.4 copy-start.6
  340.6 94.5 %collective-permute-start.2 = (bf16[2688,336]{0,1:T(8,128)(2,1)}, bf16[2688,336]{0,1:T(8,128)(2,1)}, u32[]{:S(2)}, u32[]{:S(2)}) collective-permute-start(bf16[2688,336]{0,1:T(8,128)(2,1)} %slice.24), channel_id=1, source_target_pairs={{64,0},{65,1},{66,2},{67,3},{68,4},{69,5},{70,6},{71,7},{72,8},{73... | collective-permute-start | bytes 5419016 | tf_op jit(solution)/shard_map/ppermute | solution.py:16
  343.8 52.6 %copy-start.9 = (bf16[5376,336]{0,1:T(8,128)(2,1)S(1)}, bf16[5376,336]{0,1:T(8,128)(2,1)}, u32[]{:S(2)}) copy-start(bf16[5376,336]{0,1:T(8,128)(2,1)} %copy-done.8) | copy-start | bytes 10838020
  360.5 74.6 %copy-start.7 = (bf16[5376,336]{0,1:T(8,128)(2,1)S(1)}, bf16[5376,336]{0,1:T(8,128)(2,1)}, u32[]{:S(2)}) copy-start(bf16[5376,336]{0,1:T(8,128)(2,1)} %copy-done.6) | copy-start | bytes 10838020
  396.4 41.7 %copy-start.1 = (bf16[4,2,2048]{2,1,0:T(2,128)(2,1)S(1)}, bf16[4,2,2048]{2,1,0:T(2,128)(2,1)}, u32[]{:S(2)}) copy-start(bf16[4,2,2048]{2,1,0:T(2,128)(2,1)} %param.17) | copy-start | bytes 98308
  (4 other events, 5.6 us)
Sparse Core Ops, SparseCore 0:
  15.8 94.4 all-gather.4
  192.1 92.9 all-gather.2
where the time goes:
time: 446 us; the launch traced here: 445 us
  blocking collectives  165 us (37%)
  waiting for transfers between devices  136 us (30%)
  local copies, waits for them, and re-layouts  58.1 us (13%)
  matrix products  45.2 us (10%)
  between operations  15 us (3%)
  other arithmetic  13.8 us (3%)
  starting transfers between devices  12.1 us (3%)
    psum x1, blocking collectives, local(): lax.psum((jnp.sum(member * rewards[:, None], axis=0), jnp.sum(member * (r...  165 us
    ppermute x5, waiting for transfers between devices, from_behind(): lax.ppermute(value, axis, [(source, source + steps) for source in range(i...  91.1 us
    all_gather x1, waiting for transfers between devices, local(): lax.all_gather(arrived_scaled, 'fsdp', axis=0, tiled=True)  44.6 us
    reshape x1, local copies, waits for them, and re-layouts, local(): lax.all_gather(arrived_scaled, 'fsdp', axis=0, tiled=True)  17 us
    reshape x1, local copies, waits for them, and re-layouts, local(): lax.all_gather(arrived_rows, 'fsdp', axis=0, tiled=True)  17 us
    unnamed x44, local copies, waits for them, and re-layouts  14 us
    ppermute x5, starting transfers between devices, from_behind(): lax.ppermute(value, axis, [(source, source + steps) for source in range(i...  12 us
  transfers between devices with their start and end apart: 7, of which 6 were waited for; matrix products, arithmetic and copies ran while one was open for 18% of the time, Pallas kernels for 0%

commit v1 on v0

v1 whole, which is shorter than its diff:
```python
import functools

import jax
import jax.numpy as jnp
from jax import lax
from jax.experimental import pallas as pl
from jax.experimental.pallas import tpu as pltpu
from jax.sharding import PartitionSpec as P

HEADS = 32
KV_HEADS = 16
HEAD_DIM = 128
QSCALAR = 168
GROUP = 16
GROUPS = 8
CL = 256
D = 5376
HALF = 2688
HID = 336
TOK = 16
MESH = pl.DeviceIdType.MESH
NT = (((1,), (1,)), ((), ()))


def gelu_pair(values):
    inner_arg = 0.7978845608028654 * (values + 0.044715 * values * values * values)
    tangent = jnp.tanh(inner_arg)
    result = 0.5 * values * (1.0 + tangent)
    slope_value = 0.5 * (1.0 + tangent) + 0.5 * values * (
        1.0 - tangent * tangent
    ) * 0.7978845608028654 * (1.0 + 3.0 * 0.044715 * values * values)
    return (result, slope_value)


def attend_kernel(length, query, fresh_key, fresh_value, keys, values, out, scores, probs, mixed):
    scale = float(QSCALAR) ** (-0.5)
    valid = length[pl.program_id(0)]

    def stack(ref, count):
        wide = ref[0].astype(jnp.float32)
        parts = [wide[:, j * HEAD_DIM : (j + 1) * HEAD_DIM] for j in range(count)]
        return jnp.concatenate(parts, axis=0)

    asked = stack(query, HEADS)
    new_keys = stack(fresh_key, KV_HEADS).astype(jnp.bfloat16)
    new_values = stack(fresh_value, KV_HEADS).astype(jnp.bfloat16)
    for k in range(KV_HEADS):
        scores[4 * k : 4 * k + 4, :] = lax.dot_general(
            asked[4 * k : 4 * k + 4].astype(jnp.bfloat16),
            keys[0, :, k * HEAD_DIM : (k + 1) * HEAD_DIM],
            NT,
            preferred_element_type=jnp.float32,
        )
    fresh = lax.dot_general(
        asked.astype(jnp.bfloat16), new_keys, NT, preferred_element_type=jnp.float32
    )
    row = lax.broadcasted_iota(jnp.int32, (64, 32), 0)
    column = lax.broadcasted_iota(jnp.int32, (64, 32), 1)
    seen = (lax.div(row, 4) == lax.div(column, 2)) & (lax.rem(column, 2) <= lax.rem(row, 2))
    fresh = jnp.where(seen, fresh * scale, -1e30)
    position = lax.broadcasted_iota(jnp.int32, (64, CL), 1)
    cached = jnp.where(position < valid, scores[...] * scale, -1e30)
    top = jnp.maximum(
        jnp.max(cached, axis=-1, keepdims=True), jnp.max(fresh, axis=-1, keepdims=True)
    )
    cached = jnp.exp(cached - top)
    fresh = jnp.exp(fresh - top)
    total = jnp.sum(cached, axis=-1, keepdims=True) + jnp.sum(fresh, axis=-1, keepdims=True)
    probs[...] = cached / total
    fresh = (fresh / total).astype(jnp.bfloat16)
    mixed[...] = jnp.dot(fresh, new_values, preferred_element_type=jnp.float32)
    for k in range(KV_HEADS):
        mixed[4 * k : 4 * k + 4, :] += jnp.dot(
            probs[4 * k : 4 * k + 4, :].astype(jnp.bfloat16),
            values[0, :, k * HEAD_DIM : (k + 1) * HEAD_DIM],
            preferred_element_type=jnp.float32,
        )
    done = mixed[...]
    out[0] = jnp.concatenate(
        [done[2 * j : 2 * j + 2] for j in range(HEADS)], axis=1
    ).astype(jnp.bfloat16)


def attend(queries, new_keys, new_values, cache_keys, cache_values, context_lengths):
    samples = queries.shape[0]

    def block(*shape):
        return pl.BlockSpec((1,) + shape, lambda s: (s, 0, 0))

    return pl.pallas_call(
        attend_kernel,
        grid=(samples,),
        out_shape=jax.ShapeDtypeStruct(queries.shape, jnp.bfloat16),
        in_specs=[
            pl.BlockSpec(memory_space=pltpu.SMEM),
            block(2, 4096),
            block(2, 2048),
            block(2, 2048),
            block(CL, 2048),
            block(CL, 2048),
        ],
        out_specs=block(2, 4096),
        scratch_shapes=[
            pltpu.VMEM((64, CL), jnp.float32),
            pltpu.VMEM((64, CL), jnp.float32),
            pltpu.VMEM((64, HEAD_DIM), jnp.float32),
        ],
        compiler_params=pltpu.CompilerParams(vmem_limit_bytes=24 * 1024 * 1024),
    )(context_lengths, queries, new_keys, new_values, cache_keys, cache_values)


def place():
    role = lax.axis_index("role")
    index = lax.axis_index("fsdp")
    return (
        role,
        lax.div(index, 32),
        lax.rem(lax.div(index, 8), 4),
        lax.rem(lax.div(index, 2), 4),
        lax.rem(index, 2),
    )


def device(role, high, x, y, core):
    return {"role": role, "fsdp": ((high * 4 + x) * 4 + y) * 2 + core}


def flip(bit, other):
    return lax.rem(bit + other, 2)


def turn(pos, step):
    return lax.rem(pos + step, 4)


def meet(partners):
    barrier = pltpu.get_barrier_semaphore()
    for partner in partners:
        pl.semaphore_signal(barrier, inc=1, device_id=partner, device_id_type=MESH)
    pl.semaphore_wait(barrier, len(partners))


def remote(src, dst, send, recv, target):
    return pltpu.make_async_remote_copy(
        src_ref=src,
        dst_ref=dst,
        send_sem=send,
        recv_sem=recv,
        device_id=target,
        device_id_type=MESH,
    )


def pack_kernel(
    count, reward, key, length, rows, cots,
    out_rows, out_cots, info,
    src, got, meta, token, col_send, ring_send, data_recv,
    mcol_recv, mx_send, mx_recv, my_send, my_recv,
):
    role, high, x, y, core = place()
    mine = high * 2 + core
    pos = (x, y)
    offsets = [(dr, dh, dc) for dr in (0, 1) for dh in (0, 1) for dc in (0, 1)][1:]
    column = [
        device(flip(role, dr), flip(high, dh), x, y, flip(core, dc)) for dr, dh, dc in offsets
    ]
    x_line = [device(role, high, turn(x, s), y, core) for s in (1, 2, 3)]
    y_line = [device(role, high, x, turn(y, s), core) for s in (1, 2, 3)]
    line = (x_line, y_line)
    neighbour = ((x_line[0], x_line[2]), (y_line[0], y_line[2]))
    meet(column + x_line + y_line)

    copies = []

    def send(src_ref, dst_ref, send_sem, recv_sem, target):
        copy = remote(src_ref, dst_ref, send_sem, recv_sem, target)
        copy.start()
        return copy

    def arrived(ref, sem):
        remote(ref, ref, sem, sem, x_line[0]).wait_recv()

    def column_copies():
        made = []
        for i, (dr, dh, dc) in enumerate(offsets):
            made.append(
                remote(
                    meta.at[y, x, mine], meta.at[y, x, mine],
                    col_send.at[i, 2], mcol_recv.at[mine], column[i],
                )
            )
        for i, (dr, dh, dc) in enumerate(offsets):
            part = flip(core, dc)
            for a in (0, 1):
                made.append(
                    remote(
                        src.at[a, part], got.at[a, pos[a], mine],
                        col_send.at[i, a], data_recv.at[a, pos[a], mine], column[i],
                    )
                )
        return made

    lane = lax.broadcasted_iota(jnp.int32, (8, 128), 1)
    sub = lax.broadcasted_iota(jnp.int32, (8, 128), 0)

    @pl.when(role == 0)
    def _():
        base = (lax.rem(x, 2) * 4 + mine) * TOK
        tile = jnp.zeros((8, 128), jnp.float32)
        for s in range(4):
            here = (lane >= base + 4 * s) & (lane < base + 4 * s + 4)
            live = jnp.where(s < count[0], 1.0, 0.0)
            value = jnp.where(
                sub == 0,
                reward[s],
                jnp.where(
                    sub == 1,
                    key[s].astype(jnp.float32),
                    jnp.where(
                        sub == 2,
                        length[s].astype(jnp.float32),
                        jnp.where(sub == 3, live, 0.0),
                    ),
                ),
            )
            tile = jnp.where(here, value, tile)
        meta[y, x, mine] = tile
        for a, ref in enumerate((rows, cots)):
            wide = jnp.concatenate(
                [ref[s].astype(jnp.float32) for s in range(4)], axis=0
            ).astype(jnp.bfloat16)
            src[a, 0] = wide[:, :HALF]
            src[a, 1] = wide[:, HALF:]
        for copy in column_copies():
            copy.start()
        for a in (0, 1):
            got[a, pos[a], mine] = src[a, core]

    blocks = [
        flip(high, dh) * 2 + flip(core, dc) for dh, dc in ((0, 0), (0, 1), (1, 0), (1, 1))
    ]

    def wait_column(k, what):
        if k == 0:
            @pl.when(role == 1)
            def _():
                what()
        else:
            what()

    for k, block in enumerate(blocks):
        wait_column(
            k, lambda block=block: arrived(meta.at[y, x, block], mcol_recv.at[block])
        )
    for i in range(3):
        copies.append(
            send(meta.at[y, x], meta.at[y, x], mx_send.at[i], mx_recv.at[x], x_line[i])
        )
    for k, block in enumerate(blocks):
        for a in (0, 1):
            here = got.at[a, pos[a], block]
            wait_column(
                k,
                lambda here=here, a=a, block=block: arrived(
                    here, data_recv.at[a, pos[a], block]
                ),
            )
            for way in (0, 1):
                copies.append(
                    send(
                        here, here, ring_send.at[a, way, k],
                        data_recv.at[a, pos[a], block], neighbour[a][way],
                    )
                )
    for i in (1, 2, 3):
        other = turn(x, i)
        arrived(meta.at[y, other], mx_recv.at[other])
    for i in range(3):
        copies.append(send(meta.at[y], meta.at[y], my_send.at[i], my_recv.at[y], y_line[i]))
    for i in (0, 1):
        for a in (0, 1):
            for way in (0, 1):
                origin = turn(pos[a], 3 if way == 0 else 1)
                block = 2 * i + way
                here = got.at[a, origin, block]
                arrived(here, data_recv.at[a, origin, block])
                copies.append(
                    send(
                        here, here, ring_send.at[a, way, 4 + i],
                        data_recv.at[a, origin, block], neighbour[a][way],
                    )
                )
    for i in (1, 2, 3):
        other = turn(y, i)
        arrived(meta.at[other], my_recv.at[other])

    tiles = []
    for s in range(8):
        total = jnp.zeros((8, 128), jnp.float32)
        for xi in (0, 1):
            for block in range(4):
                total = total + meta[s // 2, (s % 2) * 2 + xi, block]
        tiles.append(total)
    rewards, keys, lengths, live = (
        jnp.concatenate([t[q : q + 1] for t in tiles], axis=0) for q in range(4)
    )
    step = lax.rem(lane, 4).astype(jnp.float32)
    first = jnp.where(step == 0.0, live, 0.0)
    mean = jnp.zeros((8, 128), jnp.float32)
    denominator = jnp.ones((8, 128), jnp.float32)
    for k in range(GROUPS):
        same = keys == float(k)
        member = jnp.where(same, first, 0.0)
        group_sum = jnp.sum(member * rewards, axis=(0, 1), keepdims=True)
        group_sq = jnp.sum(member * (rewards * rewards), axis=(0, 1), keepdims=True)
        group_mean = group_sum / GROUP
        spread = group_sq / GROUP - group_mean * group_mean
        divisor = jnp.maximum(jnp.sqrt(jnp.maximum(spread, 0.0)), 1.0)
        mean = jnp.where(same, group_mean, mean)
        denominator = jnp.where(same, divisor, denominator)
    used = (live > 0.0) & (step < lengths)
    mask = jnp.where(used, 1.0, 0.0)
    weight = jnp.where(used, (rewards - mean) / denominator / jnp.maximum(lengths, 1.0), 0.0)

    a_lane = lax.broadcasted_iota(jnp.int32, (128, 128), 0)
    b_lane = lax.broadcasted_iota(jnp.int32, (128, 128), 1)
    same_column = (a_lane < 64) == (b_lane < 64)

    def count_by(take):
        return jnp.dot(
            mask.astype(jnp.bfloat16),
            jnp.where(take, 1.0, 0.0).astype(jnp.bfloat16),
            preferred_element_type=jnp.float32,
        )

    before_all = count_by(a_lane < b_lane)
    before_column = count_by((a_lane < b_lane) & same_column)
    whole = jnp.sum(mask, axis=1, keepdims=True) + jnp.zeros((8, 128), jnp.float32)
    own_column = count_by(same_column)
    rank_y_rows, rank_x_rows = [], []
    for s in range(8):
        ry = before_all[s : s + 1]
        if s % 2 == 1:
            ry = ry + whole[s - 1 : s]
        rx = before_column[s : s + 1]
        for t in range(s % 2, s, 2):
            rx = rx + own_column[t : t + 1]
        rank_y_rows.append(ry)
        rank_x_rows.append(rx)
    rank_y = jnp.concatenate(rank_y_rows, axis=0)
    rank_x = jnp.concatenate(rank_x_rows, axis=0)
    load = jnp.zeros((1, 1), jnp.float32)
    for g in range(4):
        in_y = jnp.where(lax.div(sub, 2) == g, mask, 0.0)
        in_x = jnp.where(lax.rem(sub, 2) * 2 + lax.div(lane, 64) == g, mask, 0.0)
        load = jnp.maximum(load, jnp.sum(in_y, axis=(0, 1), keepdims=True))
        load = jnp.maximum(load, jnp.sum(in_x, axis=(0, 1), keepdims=True))
    info[0] = jnp.where(used, rank_y, -1.0)
    info[1] = jnp.where(used, rank_x, -1.0)
    info[2] = mask
    info[3] = load + jnp.zeros((8, 128), jnp.float32)

    token[0] = jnp.where(used, rank_y, -1.0)
    swapped = lax.rem(x, 2) == 1
    for q, value in ((1, jnp.where(used, rank_x, -1.0)), (2, weight)):
        rolled = pltpu.roll(value, 64, 1)
        token[q] = jnp.where(swapped, rolled, value)
        token[q + 2] = jnp.where(swapped, value, rolled)

    def y_row(q):
        return jnp.concatenate(
            [token[q, pl.ds(2 * y, 1), :], token[q, pl.ds(2 * y + 1, 1), :]], axis=1
        )

    def x_row(q):
        low = lax.broadcasted_iota(jnp.int32, (1, 128), 1) < 64
        half_x = lax.div(x, 2)
        parts = [
            jnp.where(
                low,
                token[q, pl.ds(2 * t + half_x, 1), :],
                token[q + 2, pl.ds(2 * t + 2 + half_x, 1), :],
            )
            for t in (0, 2)
        ]
        return jnp.concatenate(parts, axis=1)

    target = lax.broadcasted_iota(jnp.int32, (256, 256), 0).astype(jnp.float32)
    pick_rows = jnp.where(target == y_row(0), 1.0, 0.0).astype(jnp.bfloat16)
    chosen = target == x_row(1)
    pick_cots = jnp.where(chosen, 1.0, 0.0).astype(jnp.bfloat16)
    row_weight = jnp.sum(jnp.where(chosen, x_row(2), 0.0), axis=1, keepdims=True)

    for a in (0, 1):
        for way in (0, 1):
            origin = turn(pos[a], 3 if way == 0 else 1)
            for block in range(4):
                if block % 2 != way:
                    arrived(got.at[a, origin, block], data_recv.at[a, origin, block])
        origin = turn(pos[a], 2)
        for block in range(4):
            arrived(got.at[a, origin, block], data_recv.at[a, origin, block])

    for part in range(7):
        cols = slice(part * 384, (part + 1) * 384)
        block = got[0, :, :, :, cols].reshape(256, 384)
        out_rows[:, cols] = jnp.dot(
            pick_rows, block, preferred_element_type=jnp.float32
        ).astype(jnp.bfloat16)
        block = got[1, :, :, :, cols].reshape(256, 384)
        packed = jnp.dot(pick_cots, block, preferred_element_type=jnp.float32)
        out_cots[:, cols] = (packed * row_weight).astype(jnp.bfloat16)

    for copy in copies:
        copy.wait_send()

    @pl.when(role == 0)
    def _():
        for copy in column_copies():
            copy.wait_send()


def pack(count, rewards, keys, lengths, rows, cots):
    smem = pl.BlockSpec(memory_space=pltpu.SMEM)
    vmem = pl.BlockSpec(memory_space=pltpu.VMEM)
    return pl.pallas_call(
        pack_kernel,
        out_shape=(
            jax.ShapeDtypeStruct((256, HALF), jnp.bfloat16),
            jax.ShapeDtypeStruct((256, HALF), jnp.bfloat16),
            jax.ShapeDtypeStruct((4, 8, 128), jnp.float32),
        ),
        in_specs=[smem] * 4 + [vmem] * 2,
        out_specs=(vmem, vmem, vmem),
        scratch_shapes=[
            pltpu.VMEM((2, 2, TOK, HALF), jnp.bfloat16),
            pltpu.VMEM((2, 4, 4, TOK, HALF), jnp.bfloat16),
            pltpu.VMEM((4, 4, 4, 8, 128), jnp.float32),
            pltpu.VMEM((5, 8, 128), jnp.float32),
            pltpu.SemaphoreType.DMA((7, 3)),
            pltpu.SemaphoreType.DMA((2, 2, 6)),
            pltpu.SemaphoreType.DMA((2, 4, 4)),
            pltpu.SemaphoreType.DMA((4,)),
            pltpu.SemaphoreType.DMA((3,)),
            pltpu.SemaphoreType.DMA((4,)),
            pltpu.SemaphoreType.DMA((3,)),
            pltpu.SemaphoreType.DMA((4,)),
        ],
        compiler_params=pltpu.CompilerParams(
            collective_id=1, has_side_effects=True, vmem_limit_bytes=32 * 1024 * 1024
        ),
    )(count, rewards, keys, lengths, rows, cots)


def forward_kernel(
    cap, packed_rows, packed_cots, info, w_gate, w_up, w_down,
    d_gate, d_up, hidden, out_rows, out_cots,
    held, weights, acc, row_hot, cot_hot, perm,
    own_send, relay_send, pass_send, recv, local_sem,
):
    role, high, x, y, core = place()
    pos = (y, x)
    parts = 4
    rows = cap // parts
    sibling = device(role, high, x, y, flip(core, 1))
    neighbour = (
        (device(role, high, x, turn(y, 1), core), device(role, high, x, turn(y, 3), core)),
        (device(role, high, turn(x, 1), y, core), device(role, high, turn(x, 3), y, core)),
    )
    source = (packed_rows, packed_cots)
    local = [
        pltpu.make_async_copy(source[a].at[pl.ds(0, cap)], held.at[a, core, pos[a]], local_sem.at[a])
        for a in (0, 1)
    ] + [
        pltpu.make_async_copy(w, weights.at[i], local_sem.at[2 + i])
        for i, w in enumerate((w_gate, w_up, w_down))
    ]
    for copy in local:
        copy.start()
    meet([sibling, *neighbour[0], *neighbour[1]])

    copies = []

    def send(src, a, half, group, part, send_sem, target):
        dst = held.at[a, half, group, pl.ds(part * rows, rows)]
        copy = remote(
            dst if src is None else src, dst, send_sem, recv.at[a, half, group, part], target
        )
        copy.start()
        copies.append(copy)

    def arrived(a, half, group, part):
        ref = held.at[a, half, group, pl.ds(part * rows, rows)]
        remote(ref, ref, recv.at[a, half, group, part], recv.at[a, half, group, part], sibling).wait_recv()

    for i in range(parts):
        for a in (0, 1):
            for way, part in ((0, i), (1, (i + 2) % 4), (2, i)):
                target = sibling if way == 2 else neighbour[a][way]
                src = source[a].at[pl.ds(part * rows, rows)]
                send(src, a, core, pos[a], part, own_send.at[a, way, part], target)

    other = flip(core, 1)

    def product(which, a, group):
        cols = pl.ds(pl.multiple_of(group * cap, 128), cap)
        total = None
        for half in (0, 1):
            term = lax.dot_general(
                weights[which, :, half * HALF : (half + 1) * HALF],
                held[a, half, group],
                NT,
                preferred_element_type=jnp.float32,
            )
            total = term if total is None else total + term
        acc[which, :, cols] = total

    def products(step):
        for which, a in ((0, 0), (1, 0), (2, 1)):
            product(which, a, turn(pos[a], step))

    lane = lax.broadcasted_iota(jnp.int32, (1, 128), 1)
    place_at = lax.broadcasted_iota(jnp.int32, (4 * cap, 128), 0).astype(jnp.float32)
    for s in range(8):
        cols = slice(s * 128, (s + 1) * 128)
        used = info[2, s : s + 1, :] > 0.0
        in_rows = info[0, s : s + 1, :] + float((s // 2) * cap)
        x_of = (lax.div(lane, 64) + (s % 2) * 2).astype(jnp.float32)
        in_cots = info[1, s : s + 1, :] + x_of * float(cap)
        in_rows = jnp.where(used, in_rows, -1.0)
        in_cots = jnp.where(used, in_cots, -1.0)
        row_hot[:, cols] = jnp.where(place_at == in_rows, 1.0, 0.0).astype(jnp.bfloat16)
        cot_hot[:, cols] = jnp.where(place_at == in_cots, 1.0, 0.0).astype(jnp.bfloat16)

    @pl.loop(0, 4 * cap // 128)
    def _(i):
        some = pl.ds(pl.multiple_of(i * 128, 128), 128)
        perm[some, :] = lax.dot_general(
            cot_hot[some, :], row_hot[...], NT, preferred_element_type=jnp.float32
        ).astype(jnp.bfloat16)

    for copy in local:
        copy.wait()
    for a in (0, 1):
        for part in range(parts):
            arrived(a, other, pos[a], part)
    products(0)

    for i in range(parts):
        for a in (0, 1):
            for way, part in ((0, i), (1, (i + 2) % 4)):
                group = turn(pos[a], 3 if way == 0 else 1)
                arrived(a, core, group, part)
                if i < 2:
                    send(None, a, core, group, part, relay_send.at[a, part], neighbour[a][way])
                send(None, a, core, group, part, pass_send.at[a, way, part], sibling)
    for step in (1, 3):
        for a in (0, 1):
            for part in range(parts):
                arrived(a, other, turn(pos[a], step), part)
        products(step)
    for part in (0, 2, 1, 3):
        for a in (0, 1):
            group = turn(pos[a], 2)
            arrived(a, core, group, part)
            send(None, a, core, group, part, pass_send.at[a, 2, part], sibling)
    for part in (0, 2, 1, 3):
        for a in (0, 1):
            arrived(a, other, turn(pos[a], 2), part)
    result = [
        pltpu.make_async_copy(held.at[a, role], out, local_sem.at[a])
        for a, out in ((0, out_rows), (1, out_cots))
    ]
    for copy in result:
        copy.start()
    products(2)

    for i in range(4 * cap // 128):
        cols = slice(i * 128, (i + 1) * 128)
        back = acc[2]
        upper = back.astype(jnp.bfloat16)
        lower = (back - upper.astype(jnp.float32)).astype(jnp.bfloat16)
        back = jnp.dot(upper, perm[:, cols], preferred_element_type=jnp.float32) + jnp.dot(
            lower, perm[:, cols], preferred_element_type=jnp.float32
        )
        gate = acc[0, :, cols]
        up = acc[1, :, cols]
        active, slope = gelu_pair(gate)
        d_gate[:, cols] = (back * up * slope).astype(jnp.bfloat16)
        d_up[:, cols] = (back * active).astype(jnp.bfloat16)
        row_hot[0:HID, cols] = (active * up).astype(jnp.bfloat16)
    for i in range(4 * cap // 128):
        cols = slice(i * 128, (i + 1) * 128)
        hidden[:, cols] = lax.dot_general(
            row_hot[0:HID, 0 : 4 * cap], perm[cols, :], NT, preferred_element_type=jnp.float32
        ).astype(jnp.bfloat16)

    for copy in copies:
        copy.wait_send()
    for copy in result:
        copy.wait()


def forward(cap, packed_rows, packed_cots, info, w_gate, w_up, w_down):
    vmem = pl.BlockSpec(memory_space=pltpu.VMEM)
    hbm = pl.BlockSpec(memory_space=pl.ANY)
    small = jax.ShapeDtypeStruct((HID, 4 * cap), jnp.bfloat16)
    large = jax.ShapeDtypeStruct((4, cap, HALF), jnp.bfloat16)
    d_gate, d_up, hidden, rows, cots = pl.pallas_call(
        functools.partial(forward_kernel, cap),
        out_shape=(small, small, small, large, large),
        in_specs=[hbm, hbm, vmem, hbm, hbm, hbm],
        out_specs=(vmem, vmem, vmem, hbm, hbm),
        scratch_shapes=[
            pltpu.VMEM((2, 2, 4, cap, HALF), jnp.bfloat16),
            pltpu.VMEM((3, HID, D), jnp.bfloat16),
            pltpu.VMEM((3, HID, 4 * cap), jnp.float32),
            pltpu.VMEM((4 * cap, 1024), jnp.bfloat16),
            pltpu.VMEM((4 * cap, 1024), jnp.bfloat16),
            pltpu.VMEM((4 * cap, 4 * cap), jnp.bfloat16),
            pltpu.SemaphoreType.DMA((2, 3, 4)),
            pltpu.SemaphoreType.DMA((2, 4)),
            pltpu.SemaphoreType.DMA((2, 3, 4)),
            pltpu.SemaphoreType.DMA((2, 2, 4, 4)),
            pltpu.SemaphoreType.DMA((5,)),
        ],
        compiler_params=pltpu.CompilerParams(
            collective_id=2 if cap == 128 else 3,
            has_side_effects=True,
            vmem_limit_bytes=60 * 1024 * 1024,
        ),
    )(packed_rows, packed_cots, info, w_gate, w_up, w_down)
    rows = rows.reshape(4 * cap, HALF)
    cots = cots.reshape(4 * cap, HALF)
    return tuple(
        jnp.dot(left, right, preferred_element_type=jnp.float32).astype(jnp.bfloat16)
        for left, right in ((d_gate, rows), (d_up, rows), (hidden, cots))
    )


def local(
    queries, new_keys, new_values, cache_keys, cache_values, context_lengths,
    rollout_rows, cotangents, rewards, prompt_keys, completion_lengths, finished_counts,
    gate_weight, up_weight, down_weight,
):
    attended = attend(queries, new_keys, new_values, cache_keys, cache_values, context_lengths)
    packed_rows, packed_cots, info = pack(
        finished_counts, rewards, prompt_keys, completion_lengths, rollout_rows, cotangents
    )
    operands = (packed_rows, packed_cots, info, gate_weight.T, up_weight.T, down_weight)
    grad_gate, grad_up, grad_down = lax.cond(
        info[3, 0, 0] <= 128.0,
        functools.partial(forward, 128),
        functools.partial(forward, 256),
        *operands,
    )
    return (attended, grad_gate.T, grad_up.T, grad_down)


def solution(mesh):
    return jax.shard_map(
        local,
        mesh=mesh,
        in_specs=(
            P("fsdp", None, None),
            P("fsdp", None, None),
            P("fsdp", None, None),
            P("fsdp", None, None),
            P("fsdp", None, None),
            P("fsdp"),
            P(("role", "fsdp"), None, None),
            P(("role", "fsdp"), None, None),
            P(("role", "fsdp")),
            P(("role", "fsdp")),
            P(("role", "fsdp")),
            P(("role", "fsdp")),
            P(None, "fsdp"),
            P(None, "fsdp"),
            P("fsdp", None),
        ),
        out_specs=(P("fsdp", None, None), P("role", "fsdp"), P("role", "fsdp"), P("fsdp", "role")),
        check_vma=False,
    )
```

time: 446 us -> 104 us (0.23)
  the two profiles are of different devices: /device:TPU:1 before, /device:TPU:32 now
where the time goes in v1:
time: 104 us; the launch traced here: 103 us
  Pallas kernels  84.5 us (81%)
  local copies, waits for them, and re-layouts  11.2 us (11%)
  matrix products  5.46 us (5%)
  between operations  2.03 us (2%)
    pallas_call x1, Pallas kernels, forward(): pl.pallas_call(functools.partial(forward_kernel, cap), out_shape=(small,...  40.9 us
    pallas_call x1, Pallas kernels, pack(): pl.pallas_call(pack_kernel, out_shape=(jax.ShapeDtypeStruct((256, HALF),...  39 us
    unnamed x28, local copies, waits for them, and re-layouts  10 us
    dot_general x3, matrix products, forward(): jnp.dot(left, right, preferred_element_type=jnp.float32)  5.46 us
    pallas_call x1, Pallas kernels, attend(): pl.pallas_call(attend_kernel, grid=(samples,), out_shape=jax.ShapeDtypeSt...  4.6 us

profile of v1, /device:TPU:32, one launch (start us, length us, event | category | flops | bytes accessed | tf_op | source)
XLA Modules:
  0.0 103.5 jit_solution(10444714977026465409)
XLA Ops:
  1.3 0.9 copy-done.2
  2.2 0.9 copy-done.3
  3.1 0.7 copy-done.7
  3.8 0.7 copy-done.8
  4.4 0.7 copy-done.9
  5.1 39.0 %shard_map.175 = (bf16[256,2688]{1,0:T(8,128)(2,1)S(1)}, bf16[256,2688]{1,0:T(8,128)(2,1)S(1)}, f32[4,8,128]{2,1,0:T(8,128)S(1)}) custom-call(s32[1]{0:T(128)S(6)} %copy.25.count, f32[4]{0:T(128)S(1)} %copy-done.7, s32[4]{0:T(128)S(1)} %copy-done.8, s32[4]{0:T(128)S(1)} %copy-done.9, bf16[4,4,5376]{2,1,0:T(4,128)(2,1)S(1)} %copy-done.2, ...), custom_call_target="tpu_custom_call" | custom-call | tf_op jit(solution)/shard_map/pallas_call | solution.py:426
  44.1 0.5 slice.3
  45.3 0.0 copy-start.4
  45.3 0.0 copy-start.5
  45.3 47.3 %conditional.2 = (bf16[336,2688]{1,0:T(8,128)(2,1)S(1)}, bf16[336,2688]{1,0:T(8,128)(2,1)S(1)}, bf16[336,2688]{1,0:T(8,128)(2,1)S(1)}) conditional(s32[]{:T(128)} %bitcast.4, (bf16[256,2688]{1,0:T(8,128)(2,1)S(1)}, bf16[256,2688]{1,0:T(8,128)(2,1)S(1)}, f32[4,8,128]{2,1,0:T(8,128)S(1)}, bf16[336,5376]{1,0:T(8,128)(2,1)}, bf16[336,5376]{1,0:T(8,128)(2,1)}, ...), branch_computations={%region_0.0_spmd, %region_1.0_spmd} | conditional | flops 5549064192 | bytes 68038808
  45.6 40.9 %branch_1_fun.1 = (bf16[336,512]{1,0:T(8,128)(2,1)}, bf16[336,512]{1,0:T(8,128)(2,1)}, bf16[336,512]{1,0:T(8,128)(2,1)}, bf16[4,128,2688]{2,1,0:T(8,128)(2,1)}, bf16[4,128,2688]{2,1,0:T(8,128)(2,1)}) custom-call(bf16[256,2688]{1,0:T(8,128)(2,1)S(1)} %get-tuple-element.41.packed_rows, bf16[256,2688]{1,0:T(8,128)(2,1)S(1)} %get-tuple-element.42.packed_cots, ...), custom_call_target="tpu_custom_call" | custom-call | tf_op jit(solution)/shard_map/cond/branch_1_fun/pallas_call | solution.py:609
  86.5 3.2 %fusion.4 = bf16[336,2688]{1,0:T(8,128)(2,1)S(1)} fusion(bf16[336,512]{1,0:T(8,128)(2,1)} %get-tuple-element.49, bf16[512,2688]{1,0:T(8,128)(2,1)} %bitcast.35), kind=kOutput, calls=%fused_computation.6 | convolution fusion | flops 924844032 | bytes 4902912 | tf_op jit(solution)/shard_map/cond/branch_1_fun/dot_general | solution.py:636
  89.7 1.1 %fusion.3 = bf16[336,2688]{1,0:T(8,128)(2,1)S(1)} fusion(bf16[336,512]{1,0:T(8,128)(2,1)S(1)} %copy-done.17, bf16[512,2688]{1,0:T(8,128)(2,1)S(1)} %bitcast.36), kind=kOutput, calls=%fused_computation.5 | convolution fusion | flops 924844032 | bytes 4902912 | tf_op jit(solution)/shard_map/cond/branch_1_fun/dot_general | solution.py:636
  90.8 0.6 copy-done.12
  91.4 0.0 copy-done.16
  91.5 1.1 %fusion.5 = bf16[336,2688]{1,0:T(8,128)(2,1)S(1)} fusion(bf16[336,512]{1,0:T(8,128)(2,1)S(1)} %copy-done.16, bf16[512,2688]{1,0:T(8,128)(2,1)S(1)} %bitcast.34), kind=kOutput, calls=%fused_computation.7 | convolution fusion | flops 924844032 | bytes 4902912 | tf_op jit(solution)/shard_map/cond/branch_1_fun/dot_general | solution.py:636
  92.6 0.0 copy-start.20
  92.6 0.0 copy-start.18
  92.6 0.0 copy-start.19
  92.7 1.2 %copy-done.20 = bf16[336,2688]{1,0:T(8,128)(2,1)} copy-done((bf16[336,2688]{1,0:T(8,128)(2,1)}, bf16[336,2688]{1,0:T(8,128)(2,1)S(1)}, u32[]{:S(2)}) %copy-start.20) | copy-done | bytes 1806360
  93.9 0.0 copy-start
  93.9 2.8 %copy-done = bf16[4,256,2048]{2,1,0:T(8,128)(2,1)S(1)} copy-done((bf16[4,256,2048]{2,1,0:T(8,128)(2,1)S(1)}, bf16[4,256,2048]{2,1,0:T(8,128)(2,1)}, u32[]{:S(2)}) %copy-start) | copy-done | bytes 4194328
  96.7 2.2 %copy-done.1 = bf16[4,256,2048]{2,1,0:T(8,128)(2,1)S(1)} copy-done((bf16[4,256,2048]{2,1,0:T(8,128)(2,1)S(1)}, bf16[4,256,2048]{2,1,0:T(8,128)(2,1)}, u32[]{:S(2)}) %copy-start.1) | copy-done | bytes 4194328
  98.9 4.6 %shard_map.174 = bf16[4,2,4096]{2,1,0:T(2,128)(2,1)} custom-call(s32[4]{0:T(128)S(1)} %copy-done.10, bf16[4,2,4096]{2,1,0:T(2,128)(2,1)S(1)} %copy-done.4, bf16[4,2,2048]{2,1,0:T(2,128)(2,1)S(1)} %copy-done.5, bf16[4,2,2048]{2,1,0:T(2,128)(2,1)S(1)} %copy-done.6, bf16[4,256,2048]{2,1,0:T(8,128)(2,1)S(1)} %copy-done, bf16[4,256,2048]{2,1,0:T(8,128)(2,1)S(1)} %copy-done.1), custom_call_target="tpu_custom_call" | custom-call | tf_op jit(solution)/shard_map/pallas_call | solution.py:90
  (20 shorter events, 0.0 us)
Async XLA Ops:
  1.3 0.9 copy-start.2
  2.2 0.9 copy-start.3
  3.1 0.7 copy-start.7
  3.8 0.7 copy-start.8
  4.4 0.7 copy-start.9
  45.3 48.6 %copy-start.4 = (bf16[4,2,4096]{2,1,0:T(2,128)(2,1)S(1)}, bf16[4,2,4096]{2,1,0:T(2,128)(2,1)}, u32[]{:S(2)}) copy-start(bf16[4,2,4096]{2,1,0:T(2,128)(2,1)} %query.1) | copy-start | bytes 196612
  45.3 48.6 %copy-start.5 = (bf16[4,2,2048]{2,1,0:T(2,128)(2,1)S(1)}, bf16[4,2,2048]{2,1,0:T(2,128)(2,1)}, u32[]{:S(2)}) copy-start(bf16[4,2,2048]{2,1,0:T(2,128)(2,1)} %fresh_key.1) | copy-start | bytes 98308
  45.3 48.6 %copy-start.6 = (bf16[4,2,2048]{2,1,0:T(2,128)(2,1)S(1)}, bf16[4,2,2048]{2,1,0:T(2,128)(2,1)}, u32[]{:S(2)}) copy-start(bf16[4,2,2048]{2,1,0:T(2,128)(2,1)} %fresh_value.1) | copy-start | bytes 98308
  45.3 48.6 %copy-start.10 = (s32[4]{0:T(128)S(1)}, s32[4]{0:T(128)}, u32[]{:S(2)}) copy-start(s32[4]{0:T(128)} %length.2) | copy-start | bytes 52
  86.4 3.2 %copy-start.13 = (bf16[4,128,2688]{2,1,0:T(8,128)(2,1)S(1)}, bf16[4,128,2688]{2,1,0:T(8,128)(2,1)}, u32[]{:S(2)}) copy-start(bf16[4,128,2688]{2,1,0:T(8,128)(2,1)} %get-tuple-element.48) | copy-start | bytes 8257540 | tf_op jit(solution)/shard_map/conditional
  86.5 3.2 %copy-start.17 = (bf16[336,512]{1,0:T(8,128)(2,1)S(1)}, bf16[336,512]{1,0:T(8,128)(2,1)}, u32[]{:S(2)}) copy-start(bf16[336,512]{1,0:T(8,128)(2,1)} %get-tuple-element.47) | copy-start | bytes 1032196 | tf_op jit(solution)/shard_map/conditional
  89.7 1.8 %copy-start.12 = (bf16[4,128,2688]{2,1,0:T(8,128)(2,1)S(1)}, bf16[4,128,2688]{2,1,0:T(8,128)(2,1)}, u32[]{:S(2)}) copy-start(bf16[4,128,2688]{2,1,0:T(8,128)(2,1)} %get-tuple-element.51) | copy-start | bytes 8257540 | tf_op jit(solution)/shard_map/conditional
  89.7 1.8 %copy-start.16 = (bf16[336,512]{1,0:T(8,128)(2,1)S(1)}, bf16[336,512]{1,0:T(8,128)(2,1)}, u32[]{:S(2)}) copy-start(bf16[336,512]{1,0:T(8,128)(2,1)} %get-tuple-element.50) | copy-start | bytes 1032196 | tf_op jit(solution)/shard_map/conditional
  92.6 1.2 %copy-start.20 = (bf16[336,2688]{1,0:T(8,128)(2,1)}, bf16[336,2688]{1,0:T(8,128)(2,1)S(1)}, u32[]{:S(2)}) copy-start(bf16[336,2688]{1,0:T(8,128)(2,1)S(1)} %get-tuple-element.67) | copy-start | bytes 5419012
  92.6 10.8 %copy-start.18 = (bf16[336,2688]{1,0:T(8,128)(2,1)}, bf16[336,2688]{1,0:T(8,128)(2,1)S(1)}, u32[]{:S(2)}) copy-start(bf16[336,2688]{1,0:T(8,128)(2,1)S(1)} %get-tuple-element.66) | copy-start | bytes 5419012
  92.6 10.8 %copy-start.19 = (bf16[336,2688]{1,0:T(8,128)(2,1)}, bf16[336,2688]{1,0:T(8,128)(2,1)S(1)}, u32[]{:S(2)}) copy-start(bf16[336,2688]{1,0:T(8,128)(2,1)S(1)} %get-tuple-element.65) | copy-start | bytes 5419012
  93.9 2.8 %copy-start = (bf16[4,256,2048]{2,1,0:T(8,128)(2,1)S(1)}, bf16[4,256,2048]{2,1,0:T(8,128)(2,1)}, u32[]{:S(2)}) copy-start(bf16[4,256,2048]{2,1,0:T(8,128)(2,1)} %keys.1) | copy-start | bytes 12582916
  96.7 2.2 %copy-start.1 = (bf16[4,256,2048]{2,1,0:T(8,128)(2,1)S(1)}, bf16[4,256,2048]{2,1,0:T(8,128)(2,1)}, u32[]{:S(2)}) copy-start(bf16[4,256,2048]{2,1,0:T(8,128)(2,1)} %values.1) | copy-start | bytes 12582916

commit v2 on v1

--- a/solution.py
+++ b/solution.py
@@ -32,12 +32,11 @@
     return (result, slope_value)
 
 
-def attend_kernel(length, query, fresh_key, fresh_value, keys, values, out, scores, probs, mixed):
+def attend_sample(s, valid, query, fresh_key, fresh_value, keys, values, out, scores, probs, mixed):
     scale = float(QSCALAR) ** (-0.5)
-    valid = length[pl.program_id(0)]
 
     def stack(ref, count):
-        wide = ref[0].astype(jnp.float32)
+        wide = ref[s].astype(jnp.float32)
         parts = [wide[:, j * HEAD_DIM : (j + 1) * HEAD_DIM] for j in range(count)]
         return jnp.concatenate(parts, axis=0)
 
@@ -47,7 +46,7 @@
     for k in range(KV_HEADS):
         scores[4 * k : 4 * k + 4, :] = lax.dot_general(
             asked[4 * k : 4 * k + 4].astype(jnp.bfloat16),
-            keys[0, :, k * HEAD_DIM : (k + 1) * HEAD_DIM],
+            keys[s, :, k * HEAD_DIM : (k + 1) * HEAD_DIM],
             NT,
             preferred_element_type=jnp.float32,
         )
@@ -72,41 +71,13 @@
     for k in range(KV_HEADS):
         mixed[4 * k : 4 * k + 4, :] += jnp.dot(
             probs[4 * k : 4 * k + 4, :].astype(jnp.bfloat16),
-            values[0, :, k * HEAD_DIM : (k + 1) * HEAD_DIM],
+            values[s, :, k * HEAD_DIM : (k + 1) * HEAD_DIM],
             preferred_element_type=jnp.float32,
         )
     done = mixed[...]
-    out[0] = jnp.concatenate(
+    out[s] = jnp.concatenate(
         [done[2 * j : 2 * j + 2] for j in range(HEADS)], axis=1
     ).astype(jnp.bfloat16)
-
-
-def attend(queries, new_keys, new_values, cache_keys, cache_values, context_lengths):
-    samples = queries.shape[0]
-
-    def block(*shape):
-        return pl.BlockSpec((1,) + shape, lambda s: (s, 0, 0))
-
-    return pl.pallas_call(
-        attend_kernel,
-        grid=(samples,),
-        out_shape=jax.ShapeDtypeStruct(queries.shape, jnp.bfloat16),
-        in_specs=[
-            pl.BlockSpec(memory_space=pltpu.SMEM),
-            block(2, 4096),
-            block(2, 2048),
-            block(2, 2048),
-            block(CL, 2048),
-            block(CL, 2048),
-        ],
-        out_specs=block(2, 4096),
-        scratch_shapes=[
-            pltpu.VMEM((64, CL), jnp.float32),
-            pltpu.VMEM((64, CL), jnp.float32),
-            pltpu.VMEM((64, HEAD_DIM), jnp.float32),
-        ],
-        compiler_params=pltpu.CompilerParams(vmem_limit_bytes=24 * 1024 * 1024),
-    )(context_lengths, queries, new_keys, new_values, cache_keys, cache_values)
 
 
 def place():
@@ -152,8 +123,11 @@
 
 
 def pack_kernel(
-    count, reward, key, length, rows, cots,
-    out_rows, out_cots, info,
+    count_in, reward_in, key_in, length_in, context_in, rows_in, cots_in,
+    query_in, fresh_key_in, fresh_value_in, keys_in, values_in,
+    attended, out_rows, out_cots, info,
+    count, reward, key, length, context, rows, cots, query, fresh_key, fresh_value,
+    keys, values, scores, probs, mixed, load_sem, cache_sem,
     src, got, meta, token, col_send, ring_send, data_recv,
     mcol_recv, mx_send, mx_recv, my_send, my_recv,
 ):
@@ -168,6 +142,36 @@
     y_line = [device(role, high, x, turn(y, s), core) for s in (1, 2, 3)]
     line = (x_line, y_line)
     neighbour = ((x_line[0], x_line[2]), (y_line[0], y_line[2]))
+    loads = [
+        pltpu.make_async_copy(a, b, load_sem.at[i])
+        for i, (a, b) in enumerate(
+            (
+                (count_in, count), (reward_in, reward), (key_in, key), (length_in, length),
+                (rows_in, rows), (cots_in, cots), (context_in, context), (query_in, query),
+                (fresh_key_in, fresh_key), (fresh_value_in, fresh_value),
+            )
+        )
+    ]
+    caches = [
+        [
+            pltpu.make_async_copy(a.at[s], b.at[s], cache_sem.at[s, i])
+            for i, (a, b) in enumerate(((keys_in, keys), (values_in, values)))
+        ]
+        for s in range(4)
+    ]
+    for copy in loads:
+        copy.start()
+
+    def attend(s):
+        for copy in caches[s]:
+            copy.wait()
+        attend_sample(
+            s, context[s], query, fresh_key, fresh_value, keys, values, attended,
+            scores, probs, mixed,
+        )
+
+    for copy in loads[:6]:
+        copy.wait()
     meet(column + x_line + y_line)
 
     copies = []
@@ -190,6 +194,8 @@
                 )
             )
         for i, (dr, dh, dc) in enumerate(offsets):
+            if dr == 0 and dh == 1:
+                continue
             part = flip(core, dc)
             for a in (0, 1):
                 made.append(
@@ -236,9 +242,22 @@
         for a in (0, 1):
             got[a, pos[a], mine] = src[a, core]
 
+    for pair in caches:
+        for copy in pair:
+            copy.start()
+    for copy in loads[6:]:
+        copy.wait()
+
     blocks = [
         flip(high, dh) * 2 + flip(core, dc) for dh, dc in ((0, 0), (0, 1), (1, 0), (1, 1))
     ]
+
+    def handed_on(block, k):
+        target = device(0, flip(lax.div(block, 2), 1), x, y, core)
+        here = got.at[high, jnp.where(high == 0, x, y), block]
+        return remote(
+            here, here, col_send.at[k, 0], data_recv.at[high, jnp.where(high == 0, x, y), block], target
+        )
 
     def wait_column(k, what):
         if k == 0:
@@ -257,14 +276,25 @@
             send(meta.at[y, x], meta.at[y, x], mx_send.at[i], mx_recv.at[x], x_line[i])
         )
     for k, block in enumerate(blocks):
+        @pl.when(role == 1)
+        def _():
+            arrived(
+                got.at[high, jnp.where(high == 0, x, y), block],
+                data_recv.at[high, jnp.where(high == 0, x, y), block],
+            )
+            handed_on(block, k).start()
+
         for a in (0, 1):
             here = got.at[a, pos[a], block]
-            wait_column(
-                k,
-                lambda here=here, a=a, block=block: arrived(
-                    here, data_recv.at[a, pos[a], block]
-                ),
-            )
+            if k > 0:
+                @pl.when(role == 0)
+                def _():
+                    arrived(here, data_recv.at[a, pos[a], block])
+
+            @pl.when((role == 1) & (high != a))
+            def _():
+                arrived(here, data_recv.at[a, pos[a], block])
+
             for way in (0, 1):
                 copies.append(
                     send(
@@ -272,6 +302,7 @@
                         data_recv.at[a, pos[a], block], neighbour[a][way],
                     )
                 )
+    attend(0)
     for i in (1, 2, 3):
         other = turn(x, i)
         arrived(meta.at[y, other], mx_recv.at[other])
@@ -293,6 +324,10 @@
     for i in (1, 2, 3):
         other = turn(y, i)
         arrived(meta.at[other], my_recv.at[other])
+
+    attend(1)
+    attend(2)
+    attend(3)
 
     tiles = []
     for s in range(8):
@@ -419,20 +454,43 @@
         for copy in column_copies():
             copy.wait_send()
 
-
-def pack(count, rewards, keys, lengths, rows, cots):
-    smem = pl.BlockSpec(memory_space=pltpu.SMEM)
+    @pl.when(role == 1)
+    def _():
+        for k, block in enumerate(blocks):
+            handed_on(block, k).wait_send()
+
+
+def pack(*operands):
     vmem = pl.BlockSpec(memory_space=pltpu.VMEM)
+    queries, new_keys, cache_keys = operands[7], operands[8], operands[10]
     return pl.pallas_call(
         pack_kernel,
         out_shape=(
+            jax.ShapeDtypeStruct(queries.shape, jnp.bfloat16),
             jax.ShapeDtypeStruct((256, HALF), jnp.bfloat16),
             jax.ShapeDtypeStruct((256, HALF), jnp.bfloat16),
             jax.ShapeDtypeStruct((4, 8, 128), jnp.float32),
         ),
-        in_specs=[smem] * 4 + [vmem] * 2,
-        out_specs=(vmem, vmem, vmem),
+        in_specs=[pl.BlockSpec(memory_space=pltpu.HBM)] * len(operands),
+        out_specs=(vmem, vmem, vmem, vmem),
         scratch_shapes=[
+            pltpu.SMEM((1,), jnp.int32),
+            pltpu.SMEM((4,), jnp.float32),
+            pltpu.SMEM((4,), jnp.int32),
+            pltpu.SMEM((4,), jnp.int32),
+            pltpu.SMEM((4,), jnp.int32),
+            pltpu.VMEM((4, 4, D), jnp.bfloat16),
+            pltpu.VMEM((4, 4, D), jnp.bfloat16),
+            pltpu.VMEM(queries.shape, jnp.bfloat16),
+            pltpu.VMEM(new_keys.shape, jnp.bfloat16),
+            pltpu.VMEM(new_keys.shape, jnp.bfloat16),
+            pltpu.VMEM(cache_keys.shape, jnp.bfloat16),
+            pltpu.VMEM(cache_keys.shape, jnp.bfloat16),
+            pltpu.VMEM((64, CL), jnp.float32),
+            pltpu.VMEM((64, CL), jnp.float32),
+            pltpu.VMEM((64, HEAD_DIM), jnp.float32),
+            pltpu.SemaphoreType.DMA((10,)),
+            pltpu.SemaphoreType.DMA((4, 2)),
             pltpu.VMEM((2, 2, TOK, HALF), jnp.bfloat16),
             pltpu.VMEM((2, 4, 4, TOK, HALF), jnp.bfloat16),
             pltpu.VMEM((4, 4, 4, 8, 128), jnp.float32),
@@ -447,29 +505,40 @@
             pltpu.SemaphoreType.DMA((4,)),
         ],
         compiler_params=pltpu.CompilerParams(
-            collective_id=1, has_side_effects=True, vmem_limit_bytes=32 * 1024 * 1024
+            collective_id=1, has_side_effects=True, vmem_limit_bytes=62 * 1024 * 1024
         ),
-    )(count, rewards, keys, lengths, rows, cots)
+    )(*operands)
+
+
+PARTS = 4
+EDGE = 768
+WIDE = HALF - EDGE
+ORDER = ((0, 1, 2, 3), (1, 0, 3, 2))
 
 
 def forward_kernel(
     cap, packed_rows, packed_cots, info, w_gate, w_up, w_down,
     d_gate, d_up, hidden, out_rows, out_cots,
-    held, weights, acc, row_hot, cot_hot, perm,
-    own_send, relay_send, pass_send, recv, local_sem,
+    held, weights, acc, back, row_hot, cot_hot, perm,
+    own_send, relay_send, pass_send, z_send, zpass_send,
+    ring_recv, pair_recv, z_recv, zpair_recv, local_sem, result_sem,
 ):
     role, high, x, y, core = place()
     pos = (y, x)
-    parts = 4
-    rows = cap // parts
-    sibling = device(role, high, x, y, flip(core, 1))
+    rows = cap // PARTS
+    other = flip(core, 1)
+    sibling = device(role, high, x, y, other)
     neighbour = (
         (device(role, high, x, turn(y, 1), core), device(role, high, x, turn(y, 3), core)),
         (device(role, high, turn(x, 1), y, core), device(role, high, turn(x, 3), y, core)),
     )
+    across = [device(flip(role, 1), h, x, y, core) for h in (0, 1)]
+    carried = pl.ds(pl.multiple_of(role * EDGE, 128), WIDE)
+    lent = pl.ds(pl.multiple_of(role * WIDE, 128), EDGE)
+    foreign = pl.ds(pl.multiple_of((1 - role) * WIDE, 128), EDGE)
     source = (packed_rows, packed_cots)
     local = [
-        pltpu.make_async_copy(source[a].at[pl.ds(0, cap)], held.at[a, core, pos[a]], local_sem.at[a])
+        pltpu.make_async_copy(source[a].at[pl.ds(0, cap)], held.at[a, core, 0], local_sem.at[a])
         for a in (0, 1)
     ] + [
         pltpu.make_async_copy(w, weights.at[i], local_sem.at[2 + i])
@@ -477,60 +546,140 @@
     ]
     for copy in local:
         copy.start()
-    meet([sibling, *neighbour[0], *neighbour[1]])
+    meet([sibling, *neighbour[0], *neighbour[1], *across])
 
     copies = []
 
-    def send(src, a, half, group, part, send_sem, target):
-        dst = held.at[a, half, group, pl.ds(part * rows, rows)]
-        copy = remote(
-            dst if src is None else src, dst, send_sem, recv.at[a, half, group, part], target
-        )
+    def part_of(index):
+        return lax.rem(index + 2 * high, PARTS)
+
+    def piece(part, count=1):
+        return pl.ds(pl.multiple_of(part * rows, rows), rows * count)
+
+    def send(src, dst, send_sem, recv_sem, target):
+        copy = remote(dst if src is None else src, dst, send_sem, recv_sem, target)
         copy.start()
         copies.append(copy)
 
-    def arrived(a, half, group, part):
-        ref = held.at[a, half, group, pl.ds(part * rows, rows)]
-        remote(ref, ref, recv.at[a, half, group, part], recv.at[a, half, group, part], sibling).wait_recv()
-
-    for i in range(parts):
-        for a in (0, 1):
-            for way, part in ((0, i), (1, (i + 2) % 4), (2, i)):
-                target = sibling if way == 2 else neighbour[a][way]
-                src = source[a].at[pl.ds(part * rows, rows)]
-                send(src, a, core, pos[a], part, own_send.at[a, way, part], target)
-
-    other = flip(core, 1)
-
-    def product(which, a, group):
-        cols = pl.ds(pl.multiple_of(group * cap, 128), cap)
+    def arrived(ref, sem):
+        remote(ref, ref, sem, sem, sibling).wait_recv()
+
+    for i in range(PARTS):
+        for a in (0, 1):
+            for way in (0, 1):
+                part = part_of(ORDER[way][i])
+                send(
+                    source[a].at[piece(part), carried],
+                    held.at[a, core, 1 + way, piece(part), carried],
+                    own_send.at[a, way, i], ring_recv.at[a, 1 + way, part], neighbour[a][way],
+                )
+            part = part_of(i)
+            send(
+                source[a].at[piece(part)], held.at[a, core, 0, piece(part)],
+                own_send.at[a, 2, i], pair_recv.at[a, 0, part], sibling,
+            )
+
+    def lend(a, slot, index):
+        part = part_of(index)
+        for h in (0, 1):
+            ref = held.at[a, core, slot, piece(part), lent]
+            send(None, ref, z_send.at[a, slot, index, h], z_recv.at[a, slot, part], across[h])
+
+    def hand(a, slot, index):
+        part = part_of(index)
+        ref = held.at[a, core, slot, piece(part), carried]
+        send(None, ref, pass_send.at[a, slot, index], pair_recv.at[a, slot, part], sibling)
+
+    def beside(i):
+        for a in (0, 1):
+            for way in (0, 1):
+                index = ORDER[way][i]
+                part = part_of(index)
+                ref = held.at[a, core, 1 + way, piece(part), carried]
+                arrived(ref, ring_recv.at[a, 1 + way, part])
+                if i % 2 == 0:
+                    send(
+                        ref, held.at[a, core, 3, piece(part), carried],
+                        relay_send.at[a, way, i // 2], ring_recv.at[a, 3, part], neighbour[a][way],
+                    )
+                if index < 2:
+                    lend(a, 1 + way, index)
+        for a in (0, 1):
+            for way in (0, 1):
+                hand(a, 1 + way, ORDER[way][i])
+
+    def opposite(index):
+        for a in (0, 1):
+            part = part_of(index)
+            arrived(held.at[a, core, 3, piece(part), carried], ring_recv.at[a, 3, part])
+            if index < 2:
+                lend(a, 3, index)
+        for a in (0, 1):
+            hand(a, 3, index)
+
+    def borrowed(slot):
+        for h in (0, 1):
+            for a in (0, 1):
+                for part in (2 * h, 2 * h + 1):
+                    arrived(held.at[a, core, slot, piece(part), foreign], z_recv.at[a, slot, part])
+                ref = held.at[a, core, slot, piece(2 * h, 2), foreign]
+                send(None, ref, zpass_send.at[a, slot, h], zpair_recv.at[a, slot, h], sibling)
+
+    def paired(slot):
+        for a in (0, 1):
+            for part in range(PARTS):
+                arrived(held.at[a, other, slot, piece(part), carried], pair_recv.at[a, slot, part])
+
+    def zpaired(slot):
+        for a in (0, 1):
+            for h in (0, 1):
+                arrived(
+                    held.at[a, other, slot, piece(2 * h, 2), foreign], zpair_recv.at[a, slot, h]
+                )
+
+    def product(which, slot, count):
+        a = 0 if which < 2 else 1
         total = None
         for half in (0, 1):
             term = lax.dot_general(
                 weights[which, :, half * HALF : (half + 1) * HALF],
-                held[a, half, group],
+                held[a, half, slot : slot + count].reshape(count * cap, HALF),
                 NT,
                 preferred_element_type=jnp.float32,
             )
             total = term if total is None else total + term
-        acc[which, :, cols] = total
-
-    def products(step):
-        for which, a in ((0, 0), (1, 0), (2, 1)):
-            product(which, a, turn(pos[a], step))
+        acc[which, :, slot * cap : (slot + count) * cap] = total
+
+    def partial(slot, half, start, width, first=False):
+        cols = slice(slot * cap, (slot + 1) * cap)
+        for which in range(3):
+            term = lax.dot_general(
+                weights[which, :, pl.ds(pl.multiple_of(half * HALF + start, 128), width)],
+                held[0 if which < 2 else 1, half, slot, :, pl.ds(pl.multiple_of(start, 128), width)],
+                NT,
+                preferred_element_type=jnp.float32,
+            )
+            acc[which, :, cols] = term if first else acc[which, :, cols] + term
+
+    def slot_of(line, here):
+        step = lax.rem(line - here + 4, 4)
+        return jnp.where(
+            step == 0, 0.0, jnp.where(step == 3, 1.0, jnp.where(step == 1, 2.0, 3.0))
+        )
 
     lane = lax.broadcasted_iota(jnp.int32, (1, 128), 1)
     place_at = lax.broadcasted_iota(jnp.int32, (4 * cap, 128), 0).astype(jnp.float32)
     for s in range(8):
         cols = slice(s * 128, (s + 1) * 128)
         used = info[2, s : s + 1, :] > 0.0
-        in_rows = info[0, s : s + 1, :] + float((s // 2) * cap)
-        x_of = (lax.div(lane, 64) + (s % 2) * 2).astype(jnp.float32)
-        in_cots = info[1, s : s + 1, :] + x_of * float(cap)
+        in_rows = info[0, s : s + 1, :] + slot_of(s // 2, y) * float(cap)
+        in_cots = info[1, s : s + 1, :] + slot_of(lax.div(lane, 64) + (s % 2) * 2, x) * float(cap)
         in_rows = jnp.where(used, in_rows, -1.0)
         in_cots = jnp.where(used, in_cots, -1.0)
         row_hot[:, cols] = jnp.where(place_at == in_rows, 1.0, 0.0).astype(jnp.bfloat16)
         cot_hot[:, cols] = jnp.where(place_at == in_cots, 1.0, 0.0).astype(jnp.bfloat16)
+
+    beside(0)
 
     @pl.loop(0, 4 * cap // 128)
     def _(i):
@@ -539,71 +688,96 @@
             cot_hot[some, :], row_hot[...], NT, preferred_element_type=jnp.float32
         ).astype(jnp.bfloat16)
 
+    beside(1)
+
+    def finish(slot, count):
+        cols = slice(slot * cap, (slot + count) * cap)
+        up = acc[1, :, cols]
+        active, slope = gelu_pair(acc[0, :, cols])
+        acc[0, :, cols] = active
+        acc[1, :, cols] = up * slope
+        row_hot[0:HID, cols] = (active * up).astype(jnp.bfloat16)
+
+    def spread(slot, count):
+        some = slice(slot * cap, (slot + count) * cap)
+        term = acc[2, :, some]
+        upper = term.astype(jnp.bfloat16)
+        lower = (term - upper.astype(jnp.float32)).astype(jnp.bfloat16)
+        for i in range(4 * cap // 256):
+            cols = slice(i * 256, (i + 1) * 256)
+            moved = jnp.dot(upper, perm[some, cols], preferred_element_type=jnp.float32) + jnp.dot(
+                lower, perm[some, cols], preferred_element_type=jnp.float32
+            )
+            back[:, cols] = moved if slot == 0 else back[:, cols] + moved
+
+    def results(slot, count):
+        return [
+            pltpu.make_async_copy(
+                held.at[a, role, pl.ds(slot, count)],
+                out.at[pl.ds(slot, count)],
+                result_sem.at[a, slot // 3],
+            )
+            for a, out in ((0, out_rows), (1, out_cots))
+        ]
+
     for copy in local:
         copy.wait()
     for a in (0, 1):
-        for part in range(parts):
-            arrived(a, other, pos[a], part)
-    products(0)
-
-    for i in range(parts):
-        for a in (0, 1):
-            for way, part in ((0, i), (1, (i + 2) % 4)):
-                group = turn(pos[a], 3 if way == 0 else 1)
-                arrived(a, core, group, part)
-                if i < 2:
-                    send(None, a, core, group, part, relay_send.at[a, part], neighbour[a][way])
-                send(None, a, core, group, part, pass_send.at[a, way, part], sibling)
-    for step in (1, 3):
-        for a in (0, 1):
-            for part in range(parts):
-                arrived(a, other, turn(pos[a], step), part)
-        products(step)
-    for part in (0, 2, 1, 3):
-        for a in (0, 1):
-            group = turn(pos[a], 2)
-            arrived(a, core, group, part)
-            send(None, a, core, group, part, pass_send.at[a, 2, part], sibling)
-    for part in (0, 2, 1, 3):
-        for a in (0, 1):
-            arrived(a, other, turn(pos[a], 2), part)
-    result = [
-        pltpu.make_async_copy(held.at[a, role], out, local_sem.at[a])
-        for a, out in ((0, out_rows), (1, out_cots))
-    ]
-    for copy in result:
+        for part in range(PARTS):
+            arrived(held.at[a, other, 0, piece(part)], pair_recv.at[a, 0, part])
+    for which in range(3):
+        product(which, 0, 1)
+    beside(2)
+    beside(3)
+    finish(0, 1)
+    opposite(0)
+    opposite(1)
+    spread(0, 1)
+    for slot in (1, 2):
+        borrowed(slot)
+    for slot in (1, 2):
+        paired(slot)
+    for slot in (1, 2):
+        zpaired(slot)
+    for copy in results(0, 3):
         copy.start()
-    products(2)
-
+    product(0, 1, 2)
+    product(1, 1, 2)
+    opposite(2)
+    opposite(3)
+    product(2, 1, 2)
+    finish(1, 2)
+    borrowed(3)
+    spread(1, 2)
+    partial(3, core, role * EDGE, WIDE, True)
+    partial(3, core, (1 - role) * WIDE, EDGE)
+    paired(3)
+    partial(3, other, role * EDGE, WIDE)
+    zpaired(3)
+    for copy in results(3, 1):
+        copy.start()
+    partial(3, other, (1 - role) * WIDE, EDGE)
+    finish(3, 1)
+    spread(3, 1)
     for i in range(4 * cap // 128):
         cols = slice(i * 128, (i + 1) * 128)
-        back = acc[2]
-        upper = back.astype(jnp.bfloat16)
-        lower = (back - upper.astype(jnp.float32)).astype(jnp.bfloat16)
-        back = jnp.dot(upper, perm[:, cols], preferred_element_type=jnp.float32) + jnp.dot(
-            lower, perm[:, cols], preferred_element_type=jnp.float32
-        )
-        gate = acc[0, :, cols]
-        up = acc[1, :, cols]
-        active, slope = gelu_pair(gate)
-        d_gate[:, cols] = (back * up * slope).astype(jnp.bfloat16)
-        d_up[:, cols] = (back * active).astype(jnp.bfloat16)
-        row_hot[0:HID, cols] = (active * up).astype(jnp.bfloat16)
-    for i in range(4 * cap // 128):
-        cols = slice(i * 128, (i + 1) * 128)
+        d_up[:, cols] = (back[:, cols] * acc[0, :, cols]).astype(jnp.bfloat16)
+        d_gate[:, cols] = (back[:, cols] * acc[1, :, cols]).astype(jnp.bfloat16)
+    for i in range(4 * cap // 256):
+        cols = slice(i * 256, (i + 1) * 256)
         hidden[:, cols] = lax.dot_general(
             row_hot[0:HID, 0 : 4 * cap], perm[cols, :], NT, preferred_element_type=jnp.float32
         ).astype(jnp.bfloat16)
 
     for copy in copies:
         copy.wait_send()
-    for copy in result:
+    for copy in results(0, 3) + results(3, 1):
         copy.wait()
 
 
 def forward(cap, packed_rows, packed_cots, info, w_gate, w_up, w_down):
     vmem = pl.BlockSpec(memory_space=pltpu.VMEM)
-    hbm = pl.BlockSpec(memory_space=pl.ANY)
+    hbm = pl.BlockSpec(memory_space=pltpu.HBM)
     small = jax.ShapeDtypeStruct((HID, 4 * cap), jnp.bfloat16)
     large = jax.ShapeDtypeStruct((4, cap, HALF), jnp.bfloat16)
     d_gate, d_up, hidden, rows, cots = pl.pallas_call(
@@ -615,27 +789,53 @@
             pltpu.VMEM((2, 2, 4, cap, HALF), jnp.bfloat16),
             pltpu.VMEM((3, HID, D), jnp.bfloat16),
             pltpu.VMEM((3, HID, 4 * cap), jnp.float32),
+            pltpu.VMEM((HID, 4 * cap), jnp.float32),
             pltpu.VMEM((4 * cap, 1024), jnp.bfloat16),
             pltpu.VMEM((4 * cap, 1024), jnp.bfloat16),
             pltpu.VMEM((4 * cap, 4 * cap), jnp.bfloat16),
             pltpu.SemaphoreType.DMA((2, 3, 4)),
-            pltpu.SemaphoreType.DMA((2, 4)),
-            pltpu.SemaphoreType.DMA((2, 3, 4)),
-            pltpu.SemaphoreType.DMA((2, 2, 4, 4)),
+            pltpu.SemaphoreType.DMA((2, 2, 2)),
+            pltpu.SemaphoreType.DMA((2, 4, 4)),
+            pltpu.SemaphoreType.DMA((2, 4, 2, 2)),
+            pltpu.SemaphoreType.DMA((2, 4, 2)),
+            pltpu.SemaphoreType.DMA((2, 4, 4)),
+            pltpu.SemaphoreType.DMA((2, 4, 4)),
+            pltpu.SemaphoreType.DMA((2, 4, 4)),
+            pltpu.SemaphoreType.DMA((2, 4, 2)),
             pltpu.SemaphoreType.DMA((5,)),
+            pltpu.SemaphoreType.DMA((2, 2)),
         ],
         compiler_params=pltpu.CompilerParams(
             collective_id=2 if cap == 128 else 3,
             has_side_effects=True,
-            vmem_limit_bytes=60 * 1024 * 1024,
+            vmem_limit_bytes=62 * 1024 * 1024,
         ),
     )(packed_rows, packed_cots, info, w_gate, w_up, w_down)
     rows = rows.reshape(4 * cap, HALF)
     cots = cots.reshape(4 * cap, HALF)
-    return tuple(
-        jnp.dot(left, right, preferred_element_type=jnp.float32).astype(jnp.bfloat16)
-        for left, right in ((d_gate, rows), (d_up, rows), (hidden, cots))
-    )
+    tile = 896
+    whole = pl.BlockSpec((HID, 4 * cap), lambda i: (0, 0))
+    tall = pl.BlockSpec((4 * cap, tile), lambda i: (0, i))
+    wide = pl.BlockSpec((HID, tile), lambda i: (0, i))
+    return pl.pallas_call(
+        gradient_kernel,
+        grid=(HALF // tile,),
+        out_shape=(jax.ShapeDtypeStruct((HID, HALF), jnp.bfloat16),) * 3,
+        in_specs=[whole, whole, whole, tall, tall],
+        out_specs=(wide, wide, wide),
+        compiler_params=pltpu.CompilerParams(vmem_limit_bytes=62 * 1024 * 1024),
+    )(d_gate, d_up, hidden, rows, cots)
+
+
+def gradient_kernel(d_gate, d_up, hidden, rows, cots, grad_gate, grad_up, grad_down):
+    for left, right, out in (
+        (d_gate, rows, grad_gate),
+        (d_up, rows, grad_up),
+        (hidden, cots, grad_down),
+    ):
+        out[...] = jnp.dot(left[...], right[...], preferred_element_type=jnp.float32).astype(
+            jnp.bfloat16
+        )
 
 
 def local(
@@ -643,9 +843,9 @@
     rollout_rows, cotangents, rewards, prompt_keys, completion_lengths, finished_counts,
     gate_weight, up_weight, down_weight,
 ):
-    attended = attend(queries, new_keys, new_values, cache_keys, cache_values, context_lengths)
-    packed_rows, packed_cots, info = pack(
-        finished_counts, rewards, prompt_keys, completion_lengths, rollout_rows, cotangents
+    attended, packed_rows, packed_cots, info = pack(
+        finished_counts, rewards, prompt_keys, completion_lengths, context_lengths,
+        rollout_rows, cotangents, queries, new_keys, new_values, cache_keys, cache_values,
     )
     operands = (packed_rows, packed_cots, info, gate_weight.T, up_weight.T, down_weight)
     grad_gate, grad_up, grad_down = lax.cond(

time: 104 us -> 82.2 us (0.79)
  the two profiles are of different devices: /device:TPU:32 before, /device:TPU:1 now
where the time goes in v2:
time: 82.2 us; the launch traced here: 82 us
  Pallas kernels  78.7 us (96%)
  between operations  1.95 us (2%)
  local copies, waits for them, and re-layouts  1.15 us (1%)
    pallas_call x1, Pallas kernels, pack(): pl.pallas_call(pack_kernel, out_shape=(jax.ShapeDtypeStruct(queries.shape...  36.6 us
    pallas_call x1, Pallas kernels, forward(): pl.pallas_call(functools.partial(forward_kernel, cap), out_shape=(small,...  34.8 us
    pallas_call x1, Pallas kernels, forward(): pl.pallas_call(gradient_kernel, grid=(HALF // tile,), out_shape=(jax.Shap...  7.2 us

profile of v2, /device:TPU:1, one launch (start us, length us, event | category | flops | bytes accessed | tf_op | source)
XLA Modules:
  0.0 82.0 jit_solution(15853932111531291713)
XLA Ops:
  1.3 36.6 %shard_map.174 = (bf16[4,2,4096]{2,1,0:T(2,128)(2,1)}, bf16[256,2688]{1,0:T(8,128)(2,1)S(1)}, bf16[256,2688]{1,0:T(8,128)(2,1)}, f32[4,8,128]{2,1,0:T(8,128)S(1)}) custom-call(s32[1]{0:T(128)S(6)} %copy.26.count_in, f32[4]{0:T(128)} %reward_in.1, s32[4]{0:T(128)} %key_in.1, s32[4]{0:T(128)} %length_in.1, s32[4]{0:T(128)} %context_in.1, ...), custom_call_target="tpu_custom_call" | custom-call | tf_op jit(solution)/shard_map/pallas_call | solution.py:466
  37.9 0.5 slice.3
  39.1 0.0 copy-start
  39.1 42.3 %conditional.1 = ((bf16[336,2688]{1,0:T(8,128)(2,1)}, bf16[336,2688]{1,0:T(8,128)(2,1)}, bf16[336,2688]{1,0:T(8,128)(2,1)})) conditional(s32[]{:T(128)} %bitcast.4, (bf16[256,2688]{1,0:T(8,128)(2,1)S(1)}, bf16[256,2688]{1,0:T(8,128)(2,1)}, f32[4,8,128]{2,1,0:T(8,128)S(1)}, bf16[336,5376]{1,0:T(8,128)(2,1)}, bf16[336,5376]{1,0:T(8,128)(2,1)}, ...), branch_computations={%region_0.0_spmd, %region_1.0_spmd} | conditional | bytes 8 | solution.py:851
  39.4 34.8 %branch_1_fun.2 = (bf16[336,512]{1,0:T(8,128)(2,1)}, bf16[336,512]{1,0:T(8,128)(2,1)}, bf16[336,512]{1,0:T(8,128)(2,1)}, bf16[4,128,2688]{2,1,0:T(8,128)(2,1)}, bf16[4,128,2688]{2,1,0:T(8,128)(2,1)}) custom-call(bf16[256,2688]{1,0:T(8,128)(2,1)S(1)} %get-tuple-element.35.packed_rows, bf16[256,2688]{1,0:T(8,128)(2,1)} %get-tuple-element.36.packed_cots, ...), custom_call_target="tpu_custom_call" | custom-call | tf_op jit(solution)/shard_map/cond/branch_1_fun/pallas_call | solution.py:783
  74.2 7.2 %branch_1_fun.3 = (bf16[336,2688]{1,0:T(8,128)(2,1)}, bf16[336,2688]{1,0:T(8,128)(2,1)}, bf16[336,2688]{1,0:T(8,128)(2,1)}) custom-call(bf16[336,512]{1,0:T(8,128)(2,1)} %get-tuple-element.41.d_gate, bf16[336,512]{1,0:T(8,128)(2,1)} %get-tuple-element.42.d_up, bf16[336,512]{1,0:T(8,128)(2,1)} %get-tuple-element.43.hidden, bf16[512,2688]{1,0:T(8,128)(2,1)} %bitcast.15, ...), custom_call_target="tpu_custom_call" | custom-call | tf_op jit(solution)/shard_map/cond/branch_1_fun/pallas_call | solution.py:820
  81.4 0.0 copy-done
  81.4 0.6 copy.27
Async XLA Ops:
  39.1 42.3 %copy-start = (bf16[4,2,4096]{2,1,0:T(2,128)(2,1)S(1)}, bf16[4,2,4096]{2,1,0:T(2,128)(2,1)}, u32[]{:S(2)}) copy-start(bf16[4,2,4096]{2,1,0:T(2,128)(2,1)} %get-tuple-element.74) | copy-start | bytes 196612

commit v3 on v2

--- a/solution.py
+++ b/solution.py
@@ -193,15 +193,17 @@
                     col_send.at[i, 2], mcol_recv.at[mine], column[i],
                 )
             )
-        for i, (dr, dh, dc) in enumerate(offsets):
-            if dr == 0 and dh == 1:
-                continue
-            part = flip(core, dc)
-            for a in (0, 1):
+        for step in (0, 1):
+            for i, (dr, dh, dc) in enumerate(offsets):
+                if dr == 0 and dh == 1:
+                    continue
+                part = flip(core, dc)
+                a = flip(high, dh + step)
+                spot = jnp.where(a == 0, x, y)
                 made.append(
                     remote(
-                        src.at[a, part], got.at[a, pos[a], mine],
-                        col_send.at[i, a], data_recv.at[a, pos[a], mine], column[i],
+                        src.at[a, part], got.at[a, spot, mine],
+                        col_send.at[i, a], data_recv.at[a, spot, mine], column[i],
                     )
                 )
         return made
@@ -252,12 +254,42 @@
         flip(high, dh) * 2 + flip(core, dc) for dh, dc in ((0, 0), (0, 1), (1, 0), (1, 1))
     ]
 
-    def handed_on(block, k):
-        target = device(0, flip(lax.div(block, 2), 1), x, y, core)
-        here = got.at[high, jnp.where(high == 0, x, y), block]
+    def spot_of(a):
+        return jnp.where(a == 0, x, y)
+
+    def beside(a, way):
+        step = 1 if way == 0 else 3
+        return device(
+            role, high, jnp.where(a == 0, turn(x, step), x), jnp.where(a == 0, y, turn(y, step)), core
+        )
+
+    def handed_on(k):
+        block = blocks[k]
+        here = got.at[high, spot_of(high), block]
         return remote(
-            here, here, col_send.at[k, 0], data_recv.at[high, jnp.where(high == 0, x, y), block], target
-        )
+            here, here, col_send.at[k, 0], data_recv.at[high, spot_of(high), block],
+            device(0, flip(lax.div(block, 2), 1), x, y, core),
+        )
+
+    def from_column(a, k, wait=True, hand=False):
+        block = blocks[k]
+        here = got.at[a, spot_of(a), block]
+        sem = data_recv.at[a, spot_of(a), block]
+        if wait:
+            arrived(here, sem)
+        if hand:
+            handed_on(k).start()
+        for way in (0, 1):
+            remote(here, here, ring_send.at[a, way, k], sem, beside(a, way)).start()
+
+    def relay(a, i):
+        for way in (0, 1):
+            origin = turn(spot_of(a), 3 if way == 0 else 1)
+            block = 2 * flip(high, i) + way
+            here = got.at[a, origin, block]
+            sem = data_recv.at[a, origin, block]
+            arrived(here, sem)
+            remote(here, here, ring_send.at[a, way, 4 + i], sem, beside(a, way)).start()
 
     def wait_column(k, what):
         if k == 0:
@@ -267,6 +299,17 @@
         else:
             what()
 
+    @pl.when(role == 0)
+    def _():
+        for k in (0, 1):
+            for a in (0, 1):
+                from_column(a, k, wait=k > 0)
+
+    @pl.when(role == 1)
+    def _():
+        for k in range(4):
+            from_column(high, k, hand=True)
+
     for k, block in enumerate(blocks):
         wait_column(
             k, lambda block=block: arrived(meta.at[y, x, block], mcol_recv.at[block])
@@ -275,52 +318,39 @@
         copies.append(
             send(meta.at[y, x], meta.at[y, x], mx_send.at[i], mx_recv.at[x], x_line[i])
         )
-    for k, block in enumerate(blocks):
-        @pl.when(role == 1)
-        def _():
-            arrived(
-                got.at[high, jnp.where(high == 0, x, y), block],
-                data_recv.at[high, jnp.where(high == 0, x, y), block],
-            )
-            handed_on(block, k).start()
-
+
+    @pl.when(role == 0)
+    def _():
         for a in (0, 1):
-            here = got.at[a, pos[a], block]
-            if k > 0:
-                @pl.when(role == 0)
-                def _():
-                    arrived(here, data_recv.at[a, pos[a], block])
-
-            @pl.when((role == 1) & (high != a))
-            def _():
-                arrived(here, data_recv.at[a, pos[a], block])
-
-            for way in (0, 1):
-                copies.append(
-                    send(
-                        here, here, ring_send.at[a, way, k],
-                        data_recv.at[a, pos[a], block], neighbour[a][way],
-                    )
-                )
-    attend(0)
+            relay(a, 0)
+        for k in (2, 3):
+            for a in (0, 1):
+                from_column(a, k)
+
+    @pl.when(role == 1)
+    def _():
+        for i in (0, 1):
+            for k in (2 * i, 2 * i + 1):
+                from_column(1 - high, k)
+            relay(high, i)
+
     for i in (1, 2, 3):
         other = turn(x, i)
         arrived(meta.at[y, other], mx_recv.at[other])
     for i in range(3):
         copies.append(send(meta.at[y], meta.at[y], my_send.at[i], my_recv.at[y], y_line[i]))
-    for i in (0, 1):
+
+    @pl.when(role == 0)
+    def _():
         for a in (0, 1):
-            for way in (0, 1):
-                origin = turn(pos[a], 3 if way == 0 else 1)
-                block = 2 * i + way
-                here = got.at[a, origin, block]
-                arrived(here, data_recv.at[a, origin, block])
-                copies.append(
-                    send(
-                        here, here, ring_send.at[a, way, 4 + i],
-                        data_recv.at[a, origin, block], neighbour[a][way],
-                    )
-                )
+            relay(a, 1)
+
+    @pl.when(role == 1)
+    def _():
+        for i in (0, 1):
+            relay(1 - high, i)
+
+    attend(0)
     for i in (1, 2, 3):
         other = turn(y, i)
         arrived(meta.at[other], my_recv.at[other])
@@ -448,6 +478,12 @@
 
     for copy in copies:
         copy.wait_send()
+    for a in (0, 1):
+        for way in (0, 1):
+            for k in range(6):
+                here = got.at[a, pos[a], mine]
+                sem = ring_send.at[a, way, k]
+                remote(here, here, sem, sem, beside(a, way)).wait_send()
 
     @pl.when(role == 0)
     def _():
@@ -456,8 +492,8 @@
 
     @pl.when(role == 1)
     def _():
-        for k, block in enumerate(blocks):
-            handed_on(block, k).wait_send()
+        for k in range(4):
+            handed_on(k).wait_send()
 
 
 def pack(*operands):
@@ -511,15 +547,15 @@
 
 
 PARTS = 4
-EDGE = 768
+EDGE = 896
 WIDE = HALF - EDGE
 ORDER = ((0, 1, 2, 3), (1, 0, 3, 2))
 
 
 def forward_kernel(
     cap, packed_rows, packed_cots, info, w_gate, w_up, w_down,
-    d_gate, d_up, hidden, out_rows, out_cots,
-    held, weights, acc, back, row_hot, cot_hot, perm,
+    deltas, out_rows, out_cots,
+    held, weights, acc, back, staged, row_hot, cot_hot, perm,
     own_send, relay_send, pass_send, z_send, zpass_send,
     ring_recv, pair_recv, z_recv, zpair_recv, local_sem, result_sem,
 ):
@@ -637,29 +673,25 @@
                     held.at[a, other, slot, piece(2 * h, 2), foreign], zpair_recv.at[a, slot, h]
                 )
 
+    def term(which, half, slot, count, start, width):
+        cols = pl.ds(pl.multiple_of(half * HALF + start, 128), width)
+        left = weights[which, :, cols]
+        right = held[
+            0 if which < 2 else 1, half, slot : slot + count, :, pl.ds(pl.multiple_of(start, 128), width)
+        ].reshape(count * cap, width)
+        return lax.dot_general(left, right, NT, preferred_element_type=jnp.float32)
+
+    def store(which, slot, count, value, add):
+        cols = slice(slot * cap, (slot + count) * cap)
+        acc[which, :, cols] = acc[which, :, cols] + value if add else value
+
     def product(which, slot, count):
-        a = 0 if which < 2 else 1
-        total = None
-        for half in (0, 1):
-            term = lax.dot_general(
-                weights[which, :, half * HALF : (half + 1) * HALF],
-                held[a, half, slot : slot + count].reshape(count * cap, HALF),
-                NT,
-                preferred_element_type=jnp.float32,
-            )
-            total = term if total is None else total + term
-        acc[which, :, slot * cap : (slot + count) * cap] = total
+        value = term(which, 0, slot, count, 0, HALF) + term(which, 1, slot, count, 0, HALF)
+        store(which, slot, count, value, False)
 
     def partial(slot, half, start, width, first=False):
-        cols = slice(slot * cap, (slot + 1) * cap)
-        for which in range(3):
-            term = lax.dot_general(
-                weights[which, :, pl.ds(pl.multiple_of(half * HALF + start, 128), width)],
-                held[0 if which < 2 else 1, half, slot, :, pl.ds(pl.multiple_of(start, 128), width)],
-                NT,
-                preferred_element_type=jnp.float32,
-            )
-            acc[which, :, cols] = term if first else acc[which, :, cols] + term
+        for which in (0, 1, 2):
+            store(which, slot, 1, term(which, half, slot, 1, start, width), not first)
 
     def slot_of(line, here):
         step = lax.rem(line - here + 4, 4)
@@ -761,13 +793,21 @@
     spread(3, 1)
     for i in range(4 * cap // 128):
         cols = slice(i * 128, (i + 1) * 128)
-        d_up[:, cols] = (back[:, cols] * acc[0, :, cols]).astype(jnp.bfloat16)
-        d_gate[:, cols] = (back[:, cols] * acc[1, :, cols]).astype(jnp.bfloat16)
+        staged[1, :, cols] = (back[:, cols] * acc[0, :, cols]).astype(jnp.bfloat16)
+        staged[0, :, cols] = (back[:, cols] * acc[1, :, cols]).astype(jnp.bfloat16)
+    first = pltpu.make_async_copy(
+        staged.at[pl.ds(0, 2)], deltas.at[pl.ds(0, 2)], local_sem.at[0]
+    )
+    first.start()
     for i in range(4 * cap // 256):
         cols = slice(i * 256, (i + 1) * 256)
-        hidden[:, cols] = lax.dot_general(
+        staged[2, :, cols] = lax.dot_general(
             row_hot[0:HID, 0 : 4 * cap], perm[cols, :], NT, preferred_element_type=jnp.float32
         ).astype(jnp.bfloat16)
+    second = pltpu.make_async_copy(staged.at[2], deltas.at[2], local_sem.at[1])
+    second.start()
+    first.wait()
+    second.wait()
 
     for copy in copies:
         copy.wait_send()
@@ -778,18 +818,19 @@
 def forward(cap, packed_rows, packed_cots, info, w_gate, w_up, w_down):
     vmem = pl.BlockSpec(memory_space=pltpu.VMEM)
     hbm = pl.BlockSpec(memory_space=pltpu.HBM)
-    small = jax.ShapeDtypeStruct((HID, 4 * cap), jnp.bfloat16)
+    small = jax.ShapeDtypeStruct((3, HID, 4 * cap), jnp.bfloat16)
     large = jax.ShapeDtypeStruct((4, cap, HALF), jnp.bfloat16)
-    d_gate, d_up, hidden, rows, cots = pl.pallas_call(
+    deltas, rows, cots = pl.pallas_call(
         functools.partial(forward_kernel, cap),
-        out_shape=(small, small, small, large, large),
+        out_shape=(small, large, large),
         in_specs=[hbm, hbm, vmem, hbm, hbm, hbm],
-        out_specs=(vmem, vmem, vmem, hbm, hbm),
+        out_specs=(hbm, hbm, hbm),
         scratch_shapes=[
             pltpu.VMEM((2, 2, 4, cap, HALF), jnp.bfloat16),
             pltpu.VMEM((3, HID, D), jnp.bfloat16),
             pltpu.VMEM((3, HID, 4 * cap), jnp.float32),
             pltpu.VMEM((HID, 4 * cap), jnp.float32),
+            pltpu.VMEM((3, HID, 4 * cap), jnp.bfloat16),
             pltpu.VMEM((4 * cap, 1024), jnp.bfloat16),
             pltpu.VMEM((4 * cap, 1024), jnp.bfloat16),
             pltpu.VMEM((4 * cap, 4 * cap), jnp.bfloat16),
@@ -814,26 +855,22 @@
     rows = rows.reshape(4 * cap, HALF)
     cots = cots.reshape(4 * cap, HALF)
     tile = 896
-    whole = pl.BlockSpec((HID, 4 * cap), lambda i: (0, 0))
+    whole = pl.BlockSpec((3, HID, 4 * cap), lambda i: (0, 0, 0))
     tall = pl.BlockSpec((4 * cap, tile), lambda i: (0, i))
     wide = pl.BlockSpec((HID, tile), lambda i: (0, i))
     return pl.pallas_call(
         gradient_kernel,
         grid=(HALF // tile,),
         out_shape=(jax.ShapeDtypeStruct((HID, HALF), jnp.bfloat16),) * 3,
-        in_specs=[whole, whole, whole, tall, tall],
+        in_specs=[whole, tall, tall],
         out_specs=(wide, wide, wide),
         compiler_params=pltpu.CompilerParams(vmem_limit_bytes=62 * 1024 * 1024),
-    )(d_gate, d_up, hidden, rows, cots)
-
-
-def gradient_kernel(d_gate, d_up, hidden, rows, cots, grad_gate, grad_up, grad_down):
-    for left, right, out in (
-        (d_gate, rows, grad_gate),
-        (d_up, rows, grad_up),
-        (hidden, cots, grad_down),
-    ):
-        out[...] = jnp.dot(left[...], right[...], preferred_element_type=jnp.float32).astype(
+    )(deltas, rows, cots)
+
+
+def gradient_kernel(deltas, rows, cots, grad_gate, grad_up, grad_down):
+    for g, (right, out) in enumerate(((rows, grad_gate), (rows, grad_up), (cots, grad_down))):
+        out[...] = jnp.dot(deltas[g], right[...], preferred_element_type=jnp.float32).astype(
             jnp.bfloat16
         )
 

time: 82.2 us -> 79.6 us (0.968)
  Pallas kernels: 78.7 us -> 76.1 us
    pallas_call x1, Pallas kernels: 36.6 us -> 32.8 us  [pack(): pl.pallas_call(pack_kernel, out_shape=(jax.ShapeDtypeStruct(queries.shape...]
    pallas_call x1, Pallas kernels: 34.8 us -> 36 us  [forward(): pl.pallas_call(functools.partial(forward_kernel, cap), out_shape=(small,...]
where the time goes in v3:
time: 79.6 us; the launch traced here: 79.4 us
  Pallas kernels  76.1 us (96%)
  between operations  1.95 us (2%)
  local copies, waits for them, and re-layouts  1.15 us (1%)
    pallas_call x1, Pallas kernels, forward(): pl.pallas_call(functools.partial(forward_kernel, cap), out_shape=(small,...  36 us
    pallas_call x1, Pallas kernels, pack(): pl.pallas_call(pack_kernel, out_shape=(jax.ShapeDtypeStruct(queries.shape...  32.8 us
    pallas_call x1, Pallas kernels, forward(): pl.pallas_call(gradient_kernel, grid=(HALF // tile,), out_shape=(jax.Shap...  7.23 us

profile of v3, /device:TPU:1, one launch (start us, length us, event | category | flops | bytes accessed | tf_op | source)
XLA Modules:
  0.0 79.4 jit_solution(16150063530997556200)
XLA Ops:
  1.3 32.8 %shard_map.174 = (bf16[4,2,4096]{2,1,0:T(2,128)(2,1)}, bf16[256,2688]{1,0:T(8,128)(2,1)S(1)}, bf16[256,2688]{1,0:T(8,128)(2,1)}, f32[4,8,128]{2,1,0:T(8,128)S(1)}) custom-call(s32[1]{0:T(128)S(6)} %copy.26.count_in, f32[4]{0:T(128)} %reward_in.1, s32[4]{0:T(128)} %key_in.1, s32[4]{0:T(128)} %length_in.1, s32[4]{0:T(128)} %context_in.1, ...), custom_call_target="tpu_custom_call" | custom-call | tf_op jit(solution)/shard_map/pallas_call | solution.py:502
  34.1 0.5 slice.3
  35.3 0.0 copy-start
  35.3 43.5 %conditional.1 = ((bf16[336,2688]{1,0:T(8,128)(2,1)}, bf16[336,2688]{1,0:T(8,128)(2,1)}, bf16[336,2688]{1,0:T(8,128)(2,1)})) conditional(s32[]{:T(128)} %bitcast.4, (bf16[256,2688]{1,0:T(8,128)(2,1)S(1)}, bf16[256,2688]{1,0:T(8,128)(2,1)}, f32[4,8,128]{2,1,0:T(8,128)S(1)}, bf16[336,5376]{1,0:T(8,128)(2,1)}, bf16[336,5376]{1,0:T(8,128)(2,1)}, ...), branch_computations={%region_0.0_spmd, %region_1.0_spmd} | conditional | bytes 8 | solution.py:888
  35.5 36.0 %branch_1_fun.2 = (bf16[3,336,512]{2,1,0:T(8,128)(2,1)}, bf16[4,128,2688]{2,1,0:T(8,128)(2,1)}, bf16[4,128,2688]{2,1,0:T(8,128)(2,1)}) custom-call(bf16[256,2688]{1,0:T(8,128)(2,1)S(1)} %get-tuple-element.33.packed_rows, bf16[256,2688]{1,0:T(8,128)(2,1)} %get-tuple-element.34.packed_cots, f32[4,8,128]{2,1,0:T(8,128)S(1)} %get-tuple-element.35.info, ...), custom_call_target="tpu_custom_call" | custom-call | tf_op jit(solution)/shard_map/cond/branch_1_fun/pallas_call | solution.py:823
  71.5 7.2 %branch_1_fun.3 = (bf16[336,2688]{1,0:T(8,128)(2,1)}, bf16[336,2688]{1,0:T(8,128)(2,1)}, bf16[336,2688]{1,0:T(8,128)(2,1)}) custom-call(bf16[3,336,512]{2,1,0:T(8,128)(2,1)} %get-tuple-element.39.deltas, bf16[512,2688]{1,0:T(8,128)(2,1)} %bitcast.15, bf16[512,2688]{1,0:T(8,128)(2,1)} %bitcast.16), custom_call_target="tpu_custom_call" | custom-call | tf_op jit(solution)/shard_map/cond/branch_1_fun/pallas_call | solution.py:861
  78.8 0.0 copy-done
  78.8 0.6 copy.27
Async XLA Ops:
  35.3 43.5 %copy-start = (bf16[4,2,4096]{2,1,0:T(2,128)(2,1)S(1)}, bf16[4,2,4096]{2,1,0:T(2,128)(2,1)}, u32[]{:S(2)}) copy-start(bf16[4,2,4096]{2,1,0:T(2,128)(2,1)} %get-tuple-element.70) | copy-start | bytes 196612

commit v4 on v3

--- a/solution.py
+++ b/solution.py
@@ -779,12 +779,12 @@
     opposite(3)
     product(2, 1, 2)
     finish(1, 2)
-    borrowed(3)
     spread(1, 2)
     partial(3, core, role * EDGE, WIDE, True)
-    partial(3, core, (1 - role) * WIDE, EDGE)
+    borrowed(3)
     paired(3)
     partial(3, other, role * EDGE, WIDE)
+    partial(3, core, (1 - role) * WIDE, EDGE)
     zpaired(3)
     for copy in results(3, 1):
         copy.start()

time: 79.6 us -> 79.2 us (level)
  no operation moved by 1% of the time
where the time goes in v4:
time: 79.2 us; the launch traced here: 79 us
  Pallas kernels  75.7 us (96%)
  between operations  1.95 us (2%)
  local copies, waits for them, and re-layouts  1.15 us (1%)
    pallas_call x1, Pallas kernels, forward(): pl.pallas_call(functools.partial(forward_kernel, cap), out_shape=(small,...  35.7 us
    pallas_call x1, Pallas kernels, pack(): pl.pallas_call(pack_kernel, out_shape=(jax.ShapeDtypeStruct(queries.shape...  32.8 us
    pallas_call x1, Pallas kernels, forward(): pl.pallas_call(gradient_kernel, grid=(HALF // tile,), out_shape=(jax.Shap...  7.23 us

profile of v4, /device:TPU:1, one launch (start us, length us, event | category | flops | bytes accessed | tf_op | source)
XLA Modules:
  0.0 79.0 jit_solution(14215901707300537062)
XLA Ops:
  1.3 32.8 %shard_map.174 = (bf16[4,2,4096]{2,1,0:T(2,128)(2,1)}, bf16[256,2688]{1,0:T(8,128)(2,1)S(1)}, bf16[256,2688]{1,0:T(8,128)(2,1)}, f32[4,8,128]{2,1,0:T(8,128)S(1)}) custom-call(s32[1]{0:T(128)S(6)} %copy.26.count_in, f32[4]{0:T(128)} %reward_in.1, s32[4]{0:T(128)} %key_in.1, s32[4]{0:T(128)} %length_in.1, s32[4]{0:T(128)} %context_in.1, ...), custom_call_target="tpu_custom_call" | custom-call | tf_op jit(solution)/shard_map/pallas_call | solution.py:502
  34.1 0.5 slice.3
  35.3 0.0 copy-start
  35.3 43.1 %conditional.1 = ((bf16[336,2688]{1,0:T(8,128)(2,1)}, bf16[336,2688]{1,0:T(8,128)(2,1)}, bf16[336,2688]{1,0:T(8,128)(2,1)})) conditional(s32[]{:T(128)} %bitcast.4, (bf16[256,2688]{1,0:T(8,128)(2,1)S(1)}, bf16[256,2688]{1,0:T(8,128)(2,1)}, f32[4,8,128]{2,1,0:T(8,128)S(1)}, bf16[336,5376]{1,0:T(8,128)(2,1)}, bf16[336,5376]{1,0:T(8,128)(2,1)}, ...), branch_computations={%region_0.0_spmd, %region_1.0_spmd} | conditional | bytes 8 | solution.py:888
  35.5 35.7 %branch_1_fun.2 = (bf16[3,336,512]{2,1,0:T(8,128)(2,1)}, bf16[4,128,2688]{2,1,0:T(8,128)(2,1)}, bf16[4,128,2688]{2,1,0:T(8,128)(2,1)}) custom-call(bf16[256,2688]{1,0:T(8,128)(2,1)S(1)} %get-tuple-element.33.packed_rows, bf16[256,2688]{1,0:T(8,128)(2,1)} %get-tuple-element.34.packed_cots, f32[4,8,128]{2,1,0:T(8,128)S(1)} %get-tuple-element.35.info, ...), custom_call_target="tpu_custom_call" | custom-call | tf_op jit(solution)/shard_map/cond/branch_1_fun/pallas_call | solution.py:823
  71.2 7.2 %branch_1_fun.3 = (bf16[336,2688]{1,0:T(8,128)(2,1)}, bf16[336,2688]{1,0:T(8,128)(2,1)}, bf16[336,2688]{1,0:T(8,128)(2,1)}) custom-call(bf16[3,336,512]{2,1,0:T(8,128)(2,1)} %get-tuple-element.39.deltas, bf16[512,2688]{1,0:T(8,128)(2,1)} %bitcast.15, bf16[512,2688]{1,0:T(8,128)(2,1)} %bitcast.16), custom_call_target="tpu_custom_call" | custom-call | tf_op jit(solution)/shard_map/cond/branch_1_fun/pallas_call | solution.py:861
  78.4 0.0 copy-done
  78.4 0.6 copy.27
Async XLA Ops:
  35.3 43.1 %copy-start = (bf16[4,2,4096]{2,1,0:T(2,128)(2,1)S(1)}, bf16[4,2,4096]{2,1,0:T(2,128)(2,1)}, u32[]{:S(2)}) copy-start(bf16[4,2,4096]{2,1,0:T(2,128)(2,1)} %get-tuple-element.70) | copy-start | bytes 196612
